TPU v7x, 32 devices: a whole 2x2x4 slice. The times are simulated.
32 devices in a mesh: ctx: 16 (over z, y, x), ch: 2 (over core).
Axes of the slice: x: 2, y: 2, z: 4, core: 2. Of those that a mesh axis runs over, the one named last changes fastest.
Arguments:
- first_gate: bfloat16 [2048, 8192], P('ctx', 'ch'), may hold values from -6 to 6
- second_gate: bfloat16 [2048, 8192], P('ctx', 'ch'), may hold values from -6 to 6
- output_gate: bfloat16 [2048, 8192], P('ctx', 'ch'), may hold values from -6 to 6
- values: bfloat16 [2048, 8192], P('ctx', 'ch'), may hold values from -6 to 6
- cotangent: bfloat16 [2048, 8192], P('ctx', 'ch'), may hold values from -6 to 6
- medium_filter: bfloat16 [128, 512], P(None, 'ch'), may hold values from -0.5 to 0.5
- long_filter: bfloat16 [2048, 512], P('ctx', 'ch'), may hold values from -0.088388348 to 0.088388348
Outputs:
- grad_first: bfloat16 [2048, 8192], P('ctx', 'ch')
- grad_second: bfloat16 [2048, 8192], P('ctx', 'ch')
- grad_output_gate: bfloat16 [2048, 8192], P('ctx', 'ch')
- grad_values: bfloat16 [2048, 8192], P('ctx', 'ch')
- grad_medium: float32 [128, 512], P(None, 'ch')
- grad_long: bfloat16 [2048, 512], P('ctx', 'ch')
- filter_rms: float32 [], replicated
All inputs are finite; a program needn't handle non-finite values.
Results may differ from a plain program's by a relative error of at most 0.011.
Values may be sent and summed in bfloat16 or wider, within the bound.
A program may use at most 128 MiB of HBM per device.

v0:
```python
import math

import jax
import jax.numpy as jnp
from jax import lax
from jax.sharding import PartitionSpec as P

radix_cols = 128
block_limit = 64
highest = lax.Precision.HIGHEST
wide_type = jnp.float32
narrow_type = jnp.bfloat16


def passed_along(array, axis, by):
    peers = lax.axis_size(axis)
    pairs = [(i, i + by) for i in range(peers) if 0 <= i + by < peers]
    return lax.ppermute(array, axis, pairs)


def band_table(filt, block_rows, flipped):
    tap_count, group_count = filt.shape
    window_rows = block_rows + tap_count - 1
    leading = filt[::-1] if flipped else filt
    padded = jnp.concatenate([leading.T, jnp.zeros((group_count, block_rows), filt.dtype)], axis=1)
    tiled = jnp.broadcast_to(padded[:, None, :], (group_count, block_rows, window_rows + 1))
    tiled = tiled.reshape(group_count, block_rows * (window_rows + 1))
    return tiled[:, : block_rows * window_rows].reshape(group_count, block_rows, window_rows)


def windows_of(extended, block_rows, block_count, window_rows):
    return jnp.stack(
        [
            extended[number * block_rows : number * block_rows + window_rows]
            for number in range(block_count)
        ]
    )


def phase_table(row_count, col_count, period):
    row_ids = lax.broadcasted_iota(jnp.int32, (row_count, col_count), 0)
    col_ids = lax.broadcasted_iota(jnp.int32, (row_count, col_count), 1)
    angle = (row_ids * col_ids % period).astype(wide_type) * (2.0 * math.pi / period)
    return (jnp.cos(angle), jnp.sin(angle))


def forward_dft(signal, tables):
    outer_table, cos_twist, sin_twist, forward_inner, inverse_inner = tables
    outer = jnp.einsum("kna,mnb->mkab", outer_table, signal, precision=highest)
    real_part = outer[:, 0]
    imag_part = outer[:, 1]
    twisted = jnp.stack(
        [
            real_part * cos_twist + imag_part * sin_twist,
            imag_part * cos_twist - real_part * sin_twist,
        ],
        axis=1,
    )
    return jnp.einsum("mkab,kjbq->mjaq", twisted, forward_inner, precision=highest)


def inverse_dft(spectrum, tables, total_len):
    outer_table, cos_twist, sin_twist, forward_inner, inverse_inner = tables
    inner = jnp.einsum("mkab,kjbq->mjaq", spectrum, inverse_inner, precision=highest)
    real_part = inner[:, 0]
    imag_part = inner[:, 1]
    twisted = jnp.stack(
        [
            real_part * cos_twist - imag_part * sin_twist,
            imag_part * cos_twist + real_part * sin_twist,
        ],
        axis=1,
    )
    signal = jnp.einsum("kna,mkab->mnb", outer_table, twisted, precision=highest)
    return signal / total_len


def spectral_work(pieces):
    gated_part, grad_part, filter_part = pieces
    item_count = gated_part.shape[1]
    group_size = gated_part.shape[2]
    seq_len = gated_part.shape[3]
    half_rows = seq_len // radix_cols
    full_rows = 2 * half_rows
    total_len = 2 * seq_len
    cos_outer, sin_outer = phase_table(half_rows, full_rows, full_rows)
    cos_twist, sin_twist = phase_table(full_rows, radix_cols, total_len)
    cos_inner, sin_inner = phase_table(radix_cols, radix_cols, radix_cols)
    outer_table = jnp.stack([cos_outer, -sin_outer])
    forward_inner = jnp.stack(
        [jnp.stack([cos_inner, -sin_inner]), jnp.stack([sin_inner, cos_inner])]
    )
    inverse_inner = jnp.stack(
        [jnp.stack([cos_inner, sin_inner]), jnp.stack([-sin_inner, cos_inner])]
    )
    tables = (outer_table, cos_twist, sin_twist, forward_inner, inverse_inner)
    chan_total = item_count * group_size
    shaped = (item_count, group_size, 2, full_rows, radix_cols)
    flat_shape = (chan_total, 2, full_rows, radix_cols)
    signals = jnp.concatenate(
        [
            gated_part.reshape(chan_total, half_rows, radix_cols),
            grad_part.reshape(chan_total, half_rows, radix_cols),
        ],
        axis=0,
    ).astype(wide_type)
    both_specs = forward_dft(signals, tables)
    gated_spec = both_specs[:chan_total].reshape(shaped)
    inner_spec = both_specs[chan_total:].reshape(shaped)
    filt_spec = forward_dft(
        filter_part.reshape(item_count, half_rows, radix_cols).astype(wide_type), tables
    )[:, None]
    gated_re = gated_spec[:, :, 0]
    gated_im = gated_spec[:, :, 1]
    inner_re = inner_spec[:, :, 0]
    inner_im = inner_spec[:, :, 1]
    filt_re = filt_spec[:, :, 0]
    filt_im = filt_spec[:, :, 1]
    conv_spec = jnp.stack(
        [gated_re * filt_re - gated_im * filt_im, gated_re * filt_im + gated_im * filt_re], axis=2
    )
    back_spec = jnp.stack(
        [inner_re * filt_re + inner_im * filt_im, inner_im * filt_re - inner_re * filt_im], axis=2
    )
    corr_spec = jnp.stack(
        [inner_re * gated_re + inner_im * gated_im, inner_im * gated_re - inner_re * gated_im],
        axis=2,
    )
    piece_shape = (1, item_count, group_size, seq_len)
    signals_back = inverse_dft(
        jnp.concatenate([conv_spec.reshape(flat_shape), back_spec.reshape(flat_shape)], axis=0),
        tables,
        total_len,
    )
    second_mix = signals_back[:chan_total]
    grad_carried = signals_back[chan_total:]
    scale = 1.0 / math.sqrt(seq_len * group_size)
    results = (
        second_mix.reshape(piece_shape).astype(narrow_type),
        grad_carried.reshape(piece_shape).astype(narrow_type),
    )
    summed = jnp.sum(corr_spec, axis=1)
    lagged = inverse_dft(summed, tables, total_len) * scale
    extra = lagged.reshape(1, item_count, 1, seq_len).astype(narrow_type)
    return results + (extra,)


def body(first_gate, second_gate, output_gate, values, cotangent, medium_filter, long_filter):
    tok_rows, chan_local = first_gate.shape
    tap_count, local_groups = medium_filter.shape
    group_size = chan_local // local_groups
    block_rows = math.gcd(tok_rows, block_limit)
    block_count = tok_rows // block_rows
    window_rows = block_rows + tap_count - 1
    ctx_devices = lax.axis_size("ctx")
    ctx_groups = local_groups // ctx_devices
    first_wide = first_gate.astype(wide_type)
    second_wide = second_gate.astype(wide_type)
    values_wide = values.astype(wide_type)
    cotangent_wide = cotangent.astype(wide_type)
    gated_input = (first_wide * values_wide).astype(narrow_type)
    prior_rim = passed_along(gated_input[tok_rows - tap_count + 1 :], "ctx", 1)
    extended = jnp.concatenate([prior_rim, gated_input], axis=0).reshape(
        tok_rows + tap_count - 1, local_groups, group_size
    )
    forward_win = windows_of(extended, block_rows, block_count, window_rows)
    mixed_first = jnp.einsum(
        "gij,bjgc->bigc",
        band_table(medium_filter, block_rows, True),
        forward_win,
        preferred_element_type=wide_type,
    ).reshape(tok_rows, chan_local)
    carried = (second_wide * mixed_first).astype(narrow_type)
    grad_inner = (cotangent_wide * output_gate.astype(wide_type)).astype(narrow_type)

    def channel_major(matrix, inner_size):
        return matrix.T.reshape(ctx_devices, ctx_groups, inner_size, tok_rows)

    exchanged = spectral_work(
        (
            lax.all_to_all(
                channel_major(carried, group_size), "ctx", split_axis=0, concat_axis=3, tiled=True
            ),
            lax.all_to_all(
                channel_major(grad_inner, group_size),
                "ctx",
                split_axis=0,
                concat_axis=3,
                tiled=True,
            ),
            lax.all_to_all(
                channel_major(long_filter, 1), "ctx", split_axis=0, concat_axis=3, tiled=True
            ),
        )
    )
    mix_back, carried_back, filter_back = (
        lax.all_to_all(exchanged[0], "ctx", split_axis=3, concat_axis=0, tiled=True),
        lax.all_to_all(exchanged[1], "ctx", split_axis=3, concat_axis=0, tiled=True),
        lax.all_to_all(exchanged[2], "ctx", split_axis=3, concat_axis=0, tiled=True),
    )
    grad_long = filter_back.reshape(local_groups, tok_rows).T
    second_mix = mix_back.reshape(chan_local, tok_rows).T
    grad_carried = carried_back.reshape(chan_local, tok_rows).T.astype(wide_type)
    grad_output_gate = (cotangent_wide * second_mix.astype(wide_type)).astype(narrow_type)
    grad_second = (grad_carried * mixed_first).astype(narrow_type)
    grad_mixed = (grad_carried * second_wide).astype(narrow_type)
    after_rim = passed_along(grad_mixed[: tap_count - 1], "ctx", -1)
    trailing = jnp.concatenate([grad_mixed, after_rim], axis=0).reshape(
        tok_rows + tap_count - 1, local_groups, group_size
    )
    backward_win = windows_of(trailing, block_rows, block_count, window_rows)
    grad_gated = jnp.einsum(
        "gij,bjgc->bigc",
        band_table(medium_filter, block_rows, False),
        backward_win,
        preferred_element_type=wide_type,
    ).reshape(tok_rows, chan_local)
    grad_first = (grad_gated * values_wide).astype(narrow_type)
    grad_values = (grad_gated * first_wide).astype(narrow_type)
    grad_blocks = grad_mixed.reshape(block_count, block_rows, local_groups, group_size)
    products = jnp.einsum(
        "bigc,bjgc->gij", grad_blocks, forward_win, preferred_element_type=wide_type
    )
    skewed = jnp.concatenate(
        [
            products.reshape(local_groups, block_rows * window_rows),
            jnp.zeros((local_groups, block_rows), wide_type),
        ],
        axis=1,
    )
    diagonal_sums = jnp.sum(
        skewed.reshape(local_groups, block_rows, window_rows + 1)[:, :, :tap_count], axis=1
    )
    scale = 1.0 / math.sqrt(tok_rows * ctx_devices * group_size)
    medium_terms = diagonal_sums[:, ::-1].T * scale
    grad_medium = lax.psum(medium_terms, "ctx")
    own_squares = jnp.where(lax.axis_index("ctx") == 0, jnp.sum(grad_medium * grad_medium), 0.0)
    long_squares = jnp.sum(jnp.square(grad_long.astype(wide_type)))
    total_squares = lax.psum(long_squares + own_squares, ("ctx", "ch"))
    entries = (tok_rows * ctx_devices + tap_count) * local_groups * lax.axis_size("ch")
    filter_rms = jnp.sqrt(total_squares / entries)
    return (
        grad_first,
        grad_second,
        grad_output_gate,
        grad_values,
        grad_medium,
        grad_long,
        filter_rms,
    )


def solution(mesh):
    return jax.shard_map(
        body,
        mesh=mesh,
        in_specs=(
            P("ctx", "ch"),
            P("ctx", "ch"),
            P("ctx", "ch"),
            P("ctx", "ch"),
            P("ctx", "ch"),
            P(None, "ch"),
            P("ctx", "ch"),
        ),
        out_specs=(
            P("ctx", "ch"),
            P("ctx", "ch"),
            P("ctx", "ch"),
            P("ctx", "ch"),
            P(None, "ch"),
            P("ctx", "ch"),
            P(),
        ),
        check_vma=False,
    )
```

profile of v0, /device:TPU:0, one launch (start us, length us, event | category | flops | bytes accessed | tf_op | source)
XLA Modules:
  0.0 632.6 jit_solution(4495544678841356624)
XLA Ops:
  35.8 8.4 %reshape.297 = bf16[256,64,191]{0,2,1:T(8,128)(2,1)} reshape(bf16[256,12224]{0,1:T(8,128)(2,1)} %slice.117) | data formatting | bytes 12517376 | tf_op jit(solution)/shard_map/reshape | solution.py:28
  44.3 12.2 %copy.241 = bf16[256,64,191,1]{2,1,3,0:T(8,128)(2,1)} copy(bf16[256,64,191,1]{0,2,1,3:T(8,128)(2,1)} %bitcast.223) | data formatting | bytes 12517376 | tf_op jit(solution)/shard_map/reshape | solution.py:28
  57.2 7.0 %all-to-all-start.1 = ((bf16[16,16,16,128]{3,2,1,0:T(8,128)(2,1)}), bf16[16,16,16,128]{3,2,1,0:T(8,128)(2,1)}, u32[]{:S(2)}, u32[]{:S(2)}) async-start(bf16[16,16,16,128]{3,2,1,0:T(8,128)(2,1)} %bitcast.20), calls=%async_computation.1 | async-start | bytes 2097152 | tf_op jit(solution)/shard_map/all_to_all | solution.py:184
  67.4 7.2 %fusion.21 = f32[2,64,256,16]{1,3,0,2:T(8,128)S(1)} fusion(bf16[256,64,191,1]{2,1,3,0:T(8,128)(2,1)} %copy.241, bf16[1,191,256,16]{1,3,0,2:T(8,128)(2,1)S(1)} %bitcast.229, bf16[1,191,256,16]{1,3,0,2:T(8,128)(2,1)S(1)} %bitcast.227), kind=kOutput, calls=%fused_computation.42 | convolution fusion | flops 201842688 | bytes 11485184 | tf_op jit(solution)/shard_map/gij,bjgc->bigc/dot_general | solution.py:167
  99.5 17.5 %all-to-all-done = bf16[16,16,16,128]{3,2,1,0:T(8,128)(2,1)S(1)} async-done(((bf16[16,16,16,128]{3,2,1,0:T(8,128)(2,1)}), bf16[16,16,16,128]{3,2,1,0:T(8,128)(2,1)S(1)}, u32[]{:S(2)}, u32[]{:S(2)}) %all-to-all-start) | async-done | bytes 1048608 | tf_op jit(solution)/shard_map/all_to_all | solution.py:181
  124.6 7.0 %multiply_add_fusion.1 = (f32[512,1,32,128]{3,2,1,0:T(8,128)}, f32[512,1,32,128]{3,2,1,0:T(8,128)}) fusion(f32[512,2,32,128]{3,2,1,0:T(8,128)S(1)} %convolution_bitcast_fusion, f32[32,128]{1,0:T(8,128)S(1)} %get-tuple-element.84, f32[32,128]{1,0:T(8,128)S(1)} %get-tuple-element.85), kind=kLoop, calls=%fused_computation.19 | loop fusion | flops 12582912 | bytes 33587200 | tf_op jit(solution)/shard_map/add | solution.py:54
  131.7 11.9 %pad_maximum_fusion = f32[512,2,32,128]{3,2,1,0:T(8,128)} fusion(f32[512,1,32,128]{3,2,1,0:T(8,128)} %get-tuple-element.45, f32[512,1,32,128]{3,2,1,0:T(8,128)} %get-tuple-element.44), kind=kLoop, calls=%fused_computation | loop fusion | flops 4194304 | bytes 33554432 | tf_op jit(solution)/shard_map/stack | solution.py:52
  143.5 32.6 %fusion.12 = f32[512,2,32,128]{0,3,2,1:T(8,128)} fusion(f32[512,2,32,128]{3,2,1,0:T(8,128)} %pad_maximum_fusion, f32[1,2,128,128]{2,3,0,1:T(8,128)S(1)} %get-tuple-element.77, f32[1,2,128,128]{2,3,0,1:T(8,128)S(1)} %get-tuple-element.80), kind=kOutput, calls=%fused_computation.20 | convolution fusion | flops 12884967424 | bytes 33816576 | tf_op jit(solution)/shard_map/mkab,kjbq->mjaq/dot_general | solution.py:59
  176.2 11.0 %fusion.98 = (f32[256,2,32,128]{0,3,2,1:T(8,128)}, f32[256,2,32,128]{0,3,2,1:T(8,128)}) fusion(f32[512,2,32,128]{0,3,2,1:T(8,128)} %fusion.12), kind=kLoop, calls=%fused_computation.150 | loop fusion | bytes 33554432 | tf_op jit(solution)/shard_map/slice | solution.py:108
  187.2 10.3 %copy.209 = f32[256,2,32,128]{3,2,1,0:T(8,128)} copy(f32[256,2,32,128]{0,3,2,1:T(8,128)} %get-tuple-element.48) | data formatting | bytes 16777216 | tf_op jit(solution)/shard_map/slice | solution.py:108
  197.5 10.4 %copy.217 = f32[256,2,32,128]{3,2,1,0:T(8,128)} copy(f32[256,2,32,128]{0,3,2,1:T(8,128)} %get-tuple-element.49) | data formatting | bytes 16777216 | tf_op jit(solution)/shard_map/slice | solution.py:109
  207.9 11.9 %multiply_add_fusion.2 = (f32[16,16,1,32,128]{4,3,2,1,0:T(8,128)S(1)}, f32[16,16,1,32,128]{4,3,2,1,0:T(8,128)S(1)}, f32[16,16,1,32,128]{4,3,2,1,0:T(8,128)}, f32...) fusion(f32[16,16,2,32,128]{4,3,2,1,0:T(8,128)} %bitcast.222, ...), kind=kLoop, calls=%fused_computation.29 | loop fusion | flops 18874368 | bytes 42467328 | tf_op jit(solution)/shard_map/add | solution.py:126
  223.3 11.5 %reduce = bf16[2048,16]{1,0:T(8,128)(2,1)S(1)} reduce(bf16[2048,1,1,16]{3,2,1,0:T(2,128)(2,1)S(1)} %bitcast.243, bf16[]{:T(256)} %broadcast.271), dimensions={1,2}, to_apply=%bitcast.211.reduce_sub_computation | reduce | bytes 131074
  256.2 23.9 %fusion.9 = f32[512,2,32,128]{3,2,1,0:T(8,128)S(1)} fusion(f32[512,2,32,128,1]{3,0,1,2,4:T(8,128)S(1)} %maximum_bitcast_fusion, f32[2,2,128,128]{2,3,1,0:T(8,128)S(1)} %copy-done.19), kind=kOutput, calls=%fused_computation.11 | convolution fusion | flops 12884901888 | bytes 33816576 | tf_op jit(solution)/shard_map/mkab,kjbq->mjaq/dot_general | solution.py:64
  280.1 7.0 %multiply_subtract_fusion = (f32[512,1,32,128]{3,2,1,0:T(8,128)}, f32[512,1,32,128]{3,2,1,0:T(8,128)}) fusion(f32[512,2,32,128]{3,2,1,0:T(8,128)S(1)} %fusion.9, f32[32,128]{1,0:T(8,128)S(1)} %get-tuple-element.84, f32[32,128]{1,0:T(8,128)S(1)} %get-tuple-element.85), kind=kLoop, calls=%fused_computation.17 | loop fusion | flops 12582912 | bytes 33587200 | tf_op jit(solution)/shard_map/sub | solution.py:69
  287.1 12.0 %fusion.38 = bf16[512,16,128]{2,1,0:T(8,128)(2,1)S(1)} fusion(f32[512,1,32,128]{3,2,1,0:T(8,128)} %get-tuple-element.43, f32[512,1,32,128]{3,2,1,0:T(8,128)} %get-tuple-element.42, f32[1,16,32]{2,1,0:T(8,128)S(1)} %get-tuple-element.82, f32[1,16,32]{2,1,0:T(8,128)S(1)} %get-tuple-element.83), kind=kOutput, calls=%fused_computation.61 | convolution fusion | flops 811598848 | bytes 18878464 | tf_op jit(solution)/shard_map/kna,mkab->mnb/dot_general | solution.py:74
  300.0 8.6 %copy.222 = bf16[1,16,16,2048]{2,1,0,3:T(8,128)(2,1)} copy(bf16[1,16,16,2048]{3,2,1,0:T(8,128)(2,1)S(1)} %convert_element_type.214) | data formatting | bytes 2097152 | tf_op jit(solution)/shard_map/convert_element_type | solution.py:140
  308.6 11.3 %reshape.339 = bf16[16,2,16384]{2,1,0:T(2,128)(2,1)} reshape(bf16[2048,1,16,16]{3,2,1,0:T(8,128)(2,1)} %bitcast.217) | data formatting | bytes 2097152
  319.8 7.0 %all-to-all-start.3 = ((bf16[16,2,16384]{2,1,0:T(2,128)(2,1)}), bf16[16,2,16384]{2,1,0:T(2,128)(2,1)S(1)}, u32[]{:S(2)}, u32[]{:S(2)}) async-start(bf16[16,2,16384]{2,1,0:T(2,128)(2,1)} %reshape.339), calls=%async_computation.3 | async-start | bytes 2097152 | tf_op jit(solution)/shard_map/all_to_all | solution.py:198
  330.7 8.5 %reshape.308 = bf16[256,64,191]{0,2,1:T(8,128)(2,1)} reshape(bf16[256,12224]{0,1:T(8,128)(2,1)} %slice.136) | data formatting | bytes 12517376 | tf_op jit(solution)/shard_map/reshape | solution.py:28
  339.2 12.1 %copy.251 = bf16[256,64,191,1]{2,1,3,0:T(8,128)(2,1)} copy(bf16[256,64,191,1]{0,2,1,3:T(8,128)(2,1)} %bitcast.224) | data formatting | bytes 12517376 | tf_op jit(solution)/shard_map/reshape | solution.py:28
  351.8 8.6 %copy.227 = bf16[1,16,16,2048]{2,1,0,3:T(8,128)(2,1)} copy(bf16[1,16,16,2048]{3,2,1,0:T(8,128)(2,1)S(1)} %convert_element_type.223) | data formatting | bytes 2097152 | tf_op jit(solution)/shard_map/convert_element_type | solution.py:139
  360.3 11.2 %reshape.341 = bf16[16,2,16384]{2,1,0:T(2,128)(2,1)} reshape(bf16[2048,1,16,16]{3,2,1,0:T(8,128)(2,1)} %bitcast.218) | data formatting | bytes 2097152
  381.4 8.0 %reshape.340 = bf16[2048,1,16,16]{3,2,1,0:T(8,128)(2,1)} reshape(bf16[16,2,16384]{2,1,0:T(2,128)(2,1)S(1)} %all-to-all-done.3) | data formatting | bytes 2097152
  389.4 8.3 %copy.223 = bf16[1,16,16,2048]{3,2,1,0:T(8,128)(2,1)S(1)} copy(bf16[1,16,16,2048]{2,1,0,3:T(8,128)(2,1)} %bitcast.219) | data formatting | bytes 2097152 | tf_op jit(solution)/shard_map/all_to_all | solution.py:198
  402.7 10.4 %convolution_bitcast_fusion.1 = f32[256,64,191]{2,1,0:T(8,128)} fusion(bf16[1,191,256,16]{1,3,0,2:T(8,128)(2,1)} %bitcast.230, bf16[1,191,256,16]{1,3,0,2:T(8,128)(2,1)S(1)} %bitcast.228, bf16[2,64,256,16]{1,0,3,2:T(2,128)(2,1)} %reshape.310), kind=kOutput, calls=%fused_computation.13 | convolution fusion | flops 201842688 | bytes 16695296 | tf_op jit(solution)/shard_map/bigc,bjgc->gij/dot_general | solution.py:221
  413.1 16.7 %reshape.338 = f32[256,12224]{1,0:T(8,128)} reshape(f32[256,64,191]{2,1,0:T(8,128)} %convolution_bitcast_fusion.1) | data formatting | bytes 25034752 | tf_op jit(solution)/shard_map/reshape | solution.py:226
  429.8 12.6 %copy.262 = f32[256,12224]{0,1:T(8,128)} copy(f32[256,12224]{1,0:T(8,128)} %reshape.338) | data formatting | bytes 25034752 | tf_op jit(solution)/shard_map/reshape | solution.py:226
  450.2 9.0 %reshape.342 = bf16[2048,1,16,16]{3,2,1,0:T(8,128)(2,1)} reshape(bf16[16,2,16384]{2,1,0:T(2,128)(2,1)} %all-to-all-done.4) | data formatting | bytes 2097152
  459.2 8.3 %copy.228 = bf16[1,16,16,2048]{3,2,1,0:T(8,128)(2,1)S(1)} copy(bf16[1,16,16,2048]{2,1,0,3:T(8,128)(2,1)} %bitcast.220) | data formatting | bytes 2097152 | tf_op jit(solution)/shard_map/all_to_all | solution.py:197
  470.4 84.0 %all-reduce.5.cloned.1.call-done = f32[128,256]{1,0:T(8,128)} async-done(((f32[128,256]{1,0:T(8,128)}), f32[128,256]{1,0:T(8,128)}) %all-reduce.5.cloned.1.call-update) | async-done | bytes 131088 | tf_op jit(solution)/shard_map/psum | solution.py:236
  558.6 39.6 %psum.15 = f32[]{:T(128)} all-reduce(f32[]{:T(128)S(6)} %add.148), channel_id=1, replica_groups=mesh['ctx'=16,'ch'=2] {'ctx','ch'}, use_global_device_ids=true, to_apply=%region_5.6 | all-reduce | flops 1 | bytes 8 | tf_op jit(solution)/shard_map/psum | solution.py:239
  (148 shorter events, 148.5 us)
Async XLA Ops:
  8.8 18.0 %copy-start.8 = (bf16[128,4096]{0,1:T(8,128)(2,1)}, bf16[128,4096]{0,1:T(8,128)(2,1)S(1)}, u32[]{:S(2)}) copy-start(bf16[128,4096]{0,1:T(8,128)(2,1)S(1)} %copy.200) | copy-start | bytes 3145732
  8.8 10.6 %copy-start.27 = (bf16[128,256]{1,0:T(8,128)(2,1)S(1)}, bf16[128,256]{1,0:T(8,128)(2,1)}, u32[]{:S(2)}) copy-start(bf16[128,256]{1,0:T(8,128)(2,1)} %param.13) | copy-start | bytes 196612
  10.8 18.6 %copy-start.10 = (bf16[128,4096]{0,1:T(8,128)(2,1)}, bf16[128,4096]{0,1:T(8,128)(2,1)S(1)}, u32[]{:S(2)}) copy-start(bf16[128,4096]{0,1:T(8,128)(2,1)S(1)} %copy.201) | copy-start | bytes 3145732
  13.5 18.4 %copy-start.25 = (bf16[128,256]{1,0:T(8,128)(2,1)S(1)}, bf16[128,256]{1,0:T(8,128)(2,1)}, u32[]{:S(2)}) copy-start(bf16[128,256]{1,0:T(8,128)(2,1)} %param.12) | copy-start | bytes 196612
  13.5 50.7 %collective-permute-start = (bf16[127,4096]{0,1:T(8,128)(2,1)}, bf16[127,4096]{0,1:T(8,128)(2,1)}, u32[]{:S(2)}, u32[]{:S(2)}) collective-permute-start(bf16[127,4096]{0,1:T(8,128)(2,1)} %slice.114), channel_id=1, source_target_pairs={{0,2},{2,4},{4,6},{6,8},{8,10},{10,12},{12,14},{14,16},{16,18},{18... | collective-permute-start | bytes 3121160 | tf_op jit(solution)/shard_map/ppermute | solution.py:18
  20.2 37.0 %all-to-all-start.2 = ((bf16[16,16,1,128]{3,1,2,0:T(8,128)(2,1)}), bf16[16,16,1,128]{3,1,2,0:T(8,128)(2,1)S(1)}, u32[]{:S(2)}, u32[]{:S(2)}) async-start(bf16[16,16,1,128]{3,1,2,0:T(8,128)(2,1)} %bitcast.37), calls=%async_computation.2 | async-start | bytes 131072 | tf_op jit(solution)/shard_map/all_to_all | solution.py:191
  26.8 6.0 copy-start.12
  44.3 12.2 %copy-start.21 = (bf16[128,4096]{1,0:T(8,128)(2,1)S(1)}, bf16[128,4096]{1,0:T(8,128)(2,1)}, u32[]{:S(2)}) copy-start(bf16[128,4096]{1,0:T(8,128)(2,1)} %param.8) | copy-start | bytes 3145732
  56.5 7.7 %copy-start.17 = (bf16[128,4096]{0,1:T(8,128)(2,1)S(1)}, bf16[128,4096]{0,1:T(8,128)(2,1)}, u32[]{:S(2)}) copy-start(bf16[128,4096]{0,1:T(8,128)(2,1)} %copy-done.16) | copy-start | bytes 3145732
  57.1 25.9 %copy-start.14 = (bf16[128,4096]{0,1:T(8,128)(2,1)}, bf16[128,4096]{0,1:T(8,128)(2,1)S(1)}, u32[]{:S(2)}) copy-start(bf16[128,4096]{0,1:T(8,128)(2,1)S(1)} %copy.199) | copy-start | bytes 3145732
  57.2 30.6 %all-to-all-start.1 = ((bf16[16,16,16,128]{3,2,1,0:T(8,128)(2,1)}), bf16[16,16,16,128]{3,2,1,0:T(8,128)(2,1)}, u32[]{:S(2)}, u32[]{:S(2)}) async-start(bf16[16,16,16,128]{3,2,1,0:T(8,128)(2,1)} %bitcast.20), calls=%async_computation.1 | async-start | bytes 2097152 | tf_op jit(solution)/shard_map/all_to_all | solution.py:184
  67.4 7.2 %copy-start.2 = (bf16[191,4096]{0,1:T(8,128)(2,1)}, bf16[191,4096]{0,1:T(8,128)(2,1)S(1)}, u32[]{:S(2)}) copy-start(bf16[191,4096]{0,1:T(8,128)(2,1)S(1)} %get-tuple-element.66) | copy-start | bytes 4694020
  67.4 7.2 %copy-start.4 = (bf16[191,4096]{0,1:T(8,128)(2,1)}, bf16[191,4096]{0,1:T(8,128)(2,1)S(1)}, u32[]{:S(2)}) copy-start(bf16[191,4096]{0,1:T(8,128)(2,1)S(1)} %get-tuple-element.67) | copy-start | bytes 4694020
  83.1 13.0 %copy-start = (f32[128,4096]{0,1:T(8,128)}, f32[128,4096]{0,1:T(8,128)S(1)}, u32[]{:S(2)}) copy-start(f32[128,4096]{0,1:T(8,128)S(1)} %reshape.298) | copy-start | bytes 6291460
  87.8 29.3 %all-to-all-start = ((bf16[16,16,16,128]{3,2,1,0:T(8,128)(2,1)}), bf16[16,16,16,128]{3,2,1,0:T(8,128)(2,1)S(1)}, u32[]{:S(2)}, u32[]{:S(2)}) async-start(bf16[16,16,16,128]{3,2,1,0:T(8,128)(2,1)} %bitcast.245), calls=%async_computation | async-start | bytes 2097152 | tf_op jit(solution)/shard_map/all_to_all | solution.py:181
  197.5 10.4 %copy-start.22 = (f32[16,32,128]{2,1,0:T(8,128)S(1)}, f32[16,32,128]{2,1,0:T(8,128)}, u32[]{:S(2)}) copy-start(f32[16,32,128]{2,1,0:T(8,128)} %get-tuple-element.72) | copy-start | bytes 786436
  197.5 10.4 %copy-start.23 = (f32[16,32,128]{2,1,0:T(8,128)S(1)}, f32[16,32,128]{2,1,0:T(8,128)}, u32[]{:S(2)}) copy-start(f32[16,32,128]{2,1,0:T(8,128)} %get-tuple-element.73) | copy-start | bytes 786436
  236.0 83.8 %all-to-all-start.5 = ((bf16[16,2,1024]{2,1,0:T(2,128)(2,1)}), bf16[16,2,1024]{2,1,0:T(2,128)(2,1)S(1)}, u32[]{:S(2)}, u32[]{:S(2)}) async-start(bf16[16,2,1024]{2,1,0:T(2,128)(2,1)} %reshape.343), calls=%async_computation.5 | async-start | bytes 131072 | tf_op jit(solution)/shard_map/all_to_all | solution.py:199
  242.4 4.8 copy-start.7
  247.2 2.4 copy-start.6
  249.7 2.4 copy-start.5
  254.6 1.6 copy-start.19
  308.6 18.3 %copy-start.26 = (bf16[128,256]{1,0:T(8,128)(2,1)S(1)}, bf16[128,256]{1,0:T(8,128)(2,1)}, u32[]{:S(2)}) copy-start(bf16[128,256]{1,0:T(8,128)(2,1)} %param.12) | copy-start | bytes 196612
  319.8 54.6 %all-to-all-start.3 = ((bf16[16,2,16384]{2,1,0:T(2,128)(2,1)}), bf16[16,2,16384]{2,1,0:T(2,128)(2,1)S(1)}, u32[]{:S(2)}, u32[]{:S(2)}) async-start(bf16[16,2,16384]{2,1,0:T(2,128)(2,1)} %reshape.339), calls=%async_computation.3 | async-start | bytes 2097152 | tf_op jit(solution)/shard_map/all_to_all | solution.py:198
  374.4 75.8 %all-to-all-start.4 = ((bf16[16,2,16384]{2,1,0:T(2,128)(2,1)}), bf16[16,2,16384]{2,1,0:T(2,128)(2,1)}, u32[]{:S(2)}, u32[]{:S(2)}) async-start(bf16[16,2,16384]{2,1,0:T(2,128)(2,1)} %reshape.341), calls=%async_computation.4 | async-start | bytes 2097152 | tf_op jit(solution)/shard_map/all_to_all | solution.py:197
  381.4 173.1 %all-reduce.5.cloned.1.call-start = ((), (), s32[]{:S(2)}) async-start(), calls=%async_computation.6 | async-start | bytes 262144 | tf_op jit(solution)/shard_map/psum | solution.py:236
  397.7 1.9 copy-start.15
  399.6 3.1 copy-start.3
  448.9 150.0 %collective-permute-start.1 = (bf16[127,4096]{0,1:T(8,128)(2,1)S(1)}, bf16[127,4096]{0,1:T(8,128)(2,1)}, u32[]{:S(2)}, u32[]{:S(2)}) collective-permute-start(bf16[127,4096]{0,1:T(8,128)(2,1)S(1)} %bitcast.235), channel_id=1, source_target_pairs={{2,0},{4,2},{6,4},{8,6},{10,8},{12,10},{14,12},{16,14},{18,16},{20... | collective-permute-start | bytes 3121160 | tf_op jit(solution)/shard_map/ppermute | solution.py:18
  611.7 5.6 copy-start.9
  611.7 5.6 copy-start.11
  617.2 6.6 %copy-start.24 = (f32[128,256]{1,0:T(8,128)S(1)}, f32[128,256]{1,0:T(8,128)}, u32[]{:S(2)}) copy-start(f32[128,256]{1,0:T(8,128)} %all-reduce.5.cloned.1.call-done) | copy-start | bytes 393220
  (5 other events, 6.2 us)
Sparse Core Ops, SparseCore 0:
  449.0 105.4 all-reduce.4
where the time goes:
time: 645 us; the launch traced here: 633 us
  local copies, waits for them, and re-layouts  252 us (39%)
  waiting for transfers between devices  105 us (16%)
  matrix products  101 us (16%)
  other arithmetic  71.8 us (11%)
  starting transfers between devices  45.8 us (7%)
  blocking collectives  39.6 us (6%)
  between operations  18.1 us (3%)
    psum x1, waiting for transfers between devices, body(): grad_medium = lax.psum(medium_terms, 'ctx')  84 us
    unnamed x78, local copies, waits for them, and re-layouts  62 us
    reshape x4, local copies, waits for them, and re-layouts, band_table(): tiled[:, :block_rows * window_rows]  41.2 us
    psum x1, blocking collectives, body(): total_squares = lax.psum(long_squares + own_squares, ('ctx', 'ch'))  39.6 us
    dot_general x2, matrix products, forward_dft(): jnp.einsum('mkab,kjbq->mjaq', twisted, forward_inner, precision=highest)  33.2 us
    reshape x2, local copies, waits for them, and re-layouts, body(): products.reshape(local_groups, block_rows * window_rows)  29.3 us
    dot_general x2, matrix products, inverse_dft(): jnp.einsum('mkab,kjbq->mjaq', spectrum, inverse_inner, precision=highest)  24.5 us
    slice x2, local copies, waits for them, and re-layouts, spectral_work(): gated_spec = both_specs[:chan_total].reshape(shaped)  21.4 us
  transfers between devices with their start and end apart: 9, of which 3 were waited for; matrix products, arithmetic and copies ran while one was open for 43% of the time, Pallas kernels for 0%

commit v1 on v0

v1 whole, which is shorter than its diff:
```python
import functools
import math

import jax
import jax.numpy as jnp
from jax import lax
from jax.experimental import pallas as pl
from jax.experimental.pallas import tpu as pltpu
from jax.sharding import PartitionSpec as P

wide = jnp.float32
narrow = jnp.bfloat16
params = pltpu.CompilerParams(vmem_limit_bytes=48 * 1024 * 1024)


def rolled_rows(row, rows):
    width = row.shape[1]
    base = pltpu.roll(jnp.broadcast_to(row, (16, width)), 0, 1, stride=1, stride_axis=0)
    parts = [base]
    for number in range(1, rows // 16):
        parts.append(pltpu.roll(base, 16 * number, 1))
    return jnp.concatenate([part.astype(narrow) for part in parts], axis=0)


def diagonal_sums(table):
    rows, width = table.shape
    while rows > 8:
        rows = rows // 2
        table = table[:rows] + pltpu.roll(table[rows:], width - rows, 1)
    total = table[0:1]
    for number in range(1, rows):
        total = total + pltpu.roll(table[number : number + 1], width - number, 1)
    return total


def prep_kernel(first_ref, values_ref, cotangent_ref, output_ref, gated_ref, inner_ref):
    gated = first_ref[...].astype(wide) * values_ref[...].astype(wide)
    gated_ref[...] = gated.astype(narrow).T
    inner = cotangent_ref[...].astype(wide) * output_ref[...].astype(wide)
    inner_ref[...] = inner.astype(narrow).T


def forward_kernel(size, base_ref, prior_ref, gated_ref, second_ref, mixed_ref, carried_ref):
    gate = second_ref[...].T
    for number in range(base_ref.shape[0]):
        rows = slice(number * size, (number + 1) * size)
        extended = jnp.concatenate([prior_ref[rows], gated_ref[rows]], axis=1)
        band = rolled_rows(base_ref[number : number + 1, :], gated_ref.shape[1])
        mixed = lax.dot_general(
            extended, band, (((1,), (1,)), ((), ())), preferred_element_type=wide
        )
        mixed_ref[rows] = mixed
        carried_ref[rows] = (gate[rows].astype(wide) * mixed).astype(narrow)


def filter_table(row, block):
    table = rolled_rows(row, block)
    lanes = lax.broadcasted_iota(jnp.int32, (block, block), 1)
    rows = lax.broadcasted_iota(jnp.int32, (block, block), 0)
    head = jnp.where(lanes >= rows, table[:, :block].astype(wide), 0.0).astype(narrow)
    return head, table


def back_kernel(filter_ref, inner_ref, out_ref, table_ref, pair_ref, total_ref):
    blocks, size, block = inner_ref.shape
    count = blocks * size
    head, table = filter_table(filter_ref[0], block)
    table_ref[...] = table
    table_ref[:, :block] = head
    inner = inner_ref[...].reshape(count, block)
    pair_ref[:, :block] = inner
    pair_ref[: count - size, block:] = inner[size:]
    pair_ref[count - size :, block:] = jnp.zeros((size, block), narrow)
    for lag in range(0, blocks, 2):
        rows = count - lag * size
        product = lax.dot_general(
            pair_ref[lag * size :, :],
            table_ref[:, lag * block : (lag + 2) * block],
            (((1,), (1,)), ((), ())),
            preferred_element_type=wide,
        )
        if lag == 0:
            total_ref[...] = product
        else:
            total_ref[:rows] += product
    out_ref[...] = total_ref[...].astype(narrow).reshape(blocks, size, block)


def ahead_kernel(
    scale,
    filter_ref,
    carried_ref,
    inner_ref,
    out_ref,
    long_ref,
    table_ref,
    pair_ref,
    total_ref,
    padded_ref,
    lagged_ref,
):
    blocks, size, block = inner_ref.shape
    count = blocks * size
    head, table = filter_table(filter_ref[0], block)
    table_ref[...] = table
    table_ref[:, :block] = head
    carried = carried_ref[...].reshape(count, block)
    pair_ref[:, :block] = carried
    pair_ref[size:, block:] = carried[: count - size]
    pair_ref[:size, block:] = jnp.zeros((size, block), narrow)
    padded_ref[:count] = inner_ref[...].reshape(count, block)
    padded_ref[count:] = jnp.zeros((count, block), narrow)
    for lag in range(0, blocks, 2):
        rows = count - lag * size
        weights = jnp.concatenate(
            [
                table_ref[:, lag * block : (lag + 1) * block],
                table_ref[:, (lag + 1) * block : (lag + 2) * block],
            ],
            axis=0,
        )
        product = jnp.dot(pair_ref[:rows, :], weights, preferred_element_type=wide)
        if lag == 0:
            total_ref[...] = product
        else:
            total_ref[lag * size :] += product
    out_ref[...] = total_ref[...].astype(narrow).reshape(blocks, size, block)
    turned = carried.T
    for lag in range(0, blocks, 2):
        weights = jnp.concatenate(
            [
                padded_ref[lag * size : lag * size + count],
                padded_ref[(lag + 1) * size : (lag + 1) * size + count],
            ],
            axis=1,
        )
        lagged_ref[:, lag * block : (lag + 2) * block] = jnp.dot(
            turned, weights, preferred_element_type=wide
        )
    lanes = lax.broadcasted_iota(jnp.int32, (block, block), 1)
    rows = lax.broadcasted_iota(jnp.int32, (block, block), 0)
    lagged_ref[:, :block] = jnp.where(lanes >= rows, lagged_ref[:, :block], 0.0)
    long_ref[0] = (diagonal_sums(lagged_ref[...]) * scale).astype(narrow)


def mixed_grad_kernel(
    size, back_ref, second_ref, mixed_ref, gated_ref, prior_ref, grad_second_ref, grad_mixed_ref, sums_ref
):
    tokens = second_ref.shape[0]
    back = back_ref[...].astype(wide)
    grad_second_ref[...] = (back * mixed_ref[...]).T.astype(narrow)
    grad_mixed = (back_ref[...].T.astype(wide) * second_ref[...].astype(wide)).astype(narrow)
    grad_mixed_ref[...] = grad_mixed.T
    per = 128 // size
    for number in range(sums_ref.shape[0]):
        rows = slice(number * size, (number + 1) * size)
        extended = jnp.concatenate([prior_ref[rows], gated_ref[rows]], axis=1)
        place = number % per
        pieces = []
        if place > 0:
            pieces.append(jnp.zeros((place * size, 2 * tokens), narrow))
        pieces.append(extended)
        if place < per - 1:
            pieces.append(jnp.zeros(((per - 1 - place) * size, 2 * tokens), narrow))
        weights = jnp.concatenate(pieces, axis=0)
        start = number // per * 128
        product = jnp.dot(
            grad_mixed[:, start : start + 128], weights, preferred_element_type=wide
        )
        sums_ref[number : number + 1, :] = diagonal_sums(product)


def gate_grad_kernel(
    size, base_ref, grad_mixed_ref, after_ref, first_ref, values_ref, grad_first_ref, grad_values_ref, total_ref
):
    for number in range(base_ref.shape[0]):
        rows = slice(number * size, (number + 1) * size)
        extended = jnp.concatenate([grad_mixed_ref[rows], after_ref[rows]], axis=1)
        band = rolled_rows(base_ref[number : number + 1, :], grad_mixed_ref.shape[1])
        total_ref[rows] = lax.dot_general(
            extended, band, (((1,), (1,)), ((), ())), preferred_element_type=wide
        )
    grad_gated = total_ref[...].T
    grad_first_ref[...] = (grad_gated * values_ref[...].astype(wide)).astype(narrow)
    grad_values_ref[...] = (grad_gated * first_ref[...].astype(wide)).astype(narrow)


def output_grad_kernel(ahead_ref, cotangent_ref, grad_output_ref):
    ahead = ahead_ref[...].T.astype(wide)
    grad_output_ref[...] = (cotangent_ref[...].astype(wide) * ahead).astype(narrow)


def shape_of(shape, kind):
    return jax.ShapeDtypeStruct(shape, kind)


def body(first_gate, second_gate, output_gate, values, cotangent, medium_filter, long_filter):
    tokens, channels = first_gate.shape
    taps, groups = medium_filter.shape
    size = channels // groups
    ctx = lax.axis_size("ctx")
    own = groups // ctx
    step_groups = math.gcd(groups, 16)
    width = step_groups * size
    steps = (groups // step_groups,)

    by_token = pl.BlockSpec((tokens, width), lambda i: (0, i))
    by_channel = pl.BlockSpec((width, tokens), lambda i: (i, 0))
    base_block = pl.BlockSpec((step_groups, 2 * tokens), lambda i: (i, 0))
    channel_shape = (channels, tokens)

    gated, inner = pl.pallas_call(
        prep_kernel,
        grid=steps,
        in_specs=[by_token] * 4,
        out_specs=[by_channel] * 2,
        out_shape=[shape_of(channel_shape, narrow)] * 2,
        compiler_params=params,
    )(first_gate, values, cotangent, output_gate)

    def swapped(array):
        return lax.all_to_all(array, "ctx", split_axis=0, concat_axis=0, tiled=True)

    filters = swapped(long_filter.T.reshape(ctx, own, tokens))
    inner_all = swapped(inner.reshape(ctx, own * size, tokens))
    prior = lax.ppermute(gated, "ctx", [(i, i + 1) for i in range(ctx - 1)])

    turned = medium_filter.T.astype(wide)
    pad = 2 * tokens - taps
    forward_base = jnp.concatenate(
        [
            jnp.zeros((groups, tokens + 1 - taps), wide),
            turned[:, ::-1],
            jnp.zeros((groups, tokens - 1), wide),
        ],
        axis=1,
    )
    reverse_base = jnp.concatenate([turned, jnp.zeros((groups, pad), wide)], axis=1)

    mixed, carried = pl.pallas_call(
        functools.partial(forward_kernel, size),
        grid=steps,
        in_specs=[base_block, by_channel, by_channel, by_token],
        out_specs=[by_channel] * 2,
        out_shape=[shape_of(channel_shape, wide), shape_of(channel_shape, narrow)],
        compiler_params=params,
    )(forward_base, prior, gated, second_gate)
    carried_all = swapped(carried.reshape(ctx, own * size, tokens))

    length = ctx * tokens
    filter_rows = filters.transpose(1, 0, 2).reshape(own, 1, length).astype(wide)
    row_block = pl.BlockSpec((1, 1, length), lambda g: (g, 0, 0))
    piece = pl.BlockSpec((ctx, size, tokens), lambda g: (0, g, 0))
    all_shape = (ctx, own * size, tokens)
    scratch = [
        pltpu.VMEM((tokens, length), narrow),
        pltpu.VMEM((ctx * size, 2 * tokens), narrow),
        pltpu.VMEM((ctx * size, tokens), wide),
    ]
    back_all = pl.pallas_call(
        back_kernel,
        grid=(own,),
        in_specs=[row_block, piece],
        out_specs=piece,
        out_shape=shape_of(all_shape, narrow),
        scratch_shapes=scratch,
        compiler_params=params,
    )(filter_rows, inner_all)
    back = swapped(back_all).reshape(channel_shape)

    scale = 1.0 / math.sqrt(length * size)
    ahead_all, long_rows = pl.pallas_call(
        functools.partial(ahead_kernel, scale),
        grid=(own,),
        in_specs=[row_block, piece, piece],
        out_specs=[piece, row_block],
        out_shape=[shape_of(all_shape, narrow), shape_of((own, 1, length), narrow)],
        scratch_shapes=scratch
        + [
            pltpu.VMEM((2 * ctx * size, tokens), narrow),
            pltpu.VMEM((tokens, length), wide),
        ],
        compiler_params=params,
    )(filter_rows, carried_all, inner_all)
    ahead = swapped(ahead_all).reshape(channel_shape)
    long_pieces = long_rows.reshape(own, ctx, tokens).transpose(1, 0, 2)
    grad_long = swapped(long_pieces).reshape(groups, tokens).T

    grad_second, grad_mixed, sums = pl.pallas_call(
        functools.partial(mixed_grad_kernel, size),
        grid=steps,
        in_specs=[by_channel, by_token, by_channel, by_channel, by_channel],
        out_specs=[by_token, by_channel, base_block],
        out_shape=[
            shape_of((tokens, channels), narrow),
            shape_of(channel_shape, narrow),
            shape_of((groups, 2 * tokens), wide),
        ],
        compiler_params=params,
    )(back, second_gate, mixed, gated, prior)
    after = lax.ppermute(grad_mixed, "ctx", [(i + 1, i) for i in range(ctx - 1)])

    terms = sums[:, tokens + 1 - taps : tokens + 1][:, ::-1] * scale
    medium_own = jnp.sum(swapped(terms.reshape(ctx, own, taps)), axis=0)
    squares = jnp.sum(jnp.square(medium_own)) + jnp.sum(jnp.square(long_rows.astype(wide)))
    package = jnp.concatenate([medium_own, jnp.full((1, taps), squares, wide)], axis=0)
    gathered = swapped(jnp.broadcast_to(package[None], (ctx, own + 1, taps)))
    grad_medium = gathered[:, :own].reshape(groups, taps).T
    ch = lax.axis_size("ch")
    side = jnp.broadcast_to(jnp.sum(gathered[:, own], axis=0)[None, None], (ch, 1, taps))
    total = jnp.sum(
        lax.all_to_all(side, "ch", split_axis=0, concat_axis=0, tiled=True), axis=0
    )[0, 0]
    filter_rms = jnp.sqrt(total / ((length + taps) * groups * ch))

    grad_first, grad_values = pl.pallas_call(
        functools.partial(gate_grad_kernel, size),
        grid=steps,
        in_specs=[base_block, by_channel, by_channel, by_token, by_token],
        out_specs=[by_token] * 2,
        out_shape=[shape_of((tokens, channels), narrow)] * 2,
        scratch_shapes=[pltpu.VMEM((width, tokens), wide)],
        compiler_params=params,
    )(reverse_base, grad_mixed, after, first_gate, values)
    grad_output_gate = pl.pallas_call(
        output_grad_kernel,
        grid=steps,
        in_specs=[by_channel, by_token],
        out_specs=by_token,
        out_shape=shape_of((tokens, channels), narrow),
        compiler_params=params,
    )(ahead, cotangent)
    return (
        grad_first,
        grad_second,
        grad_output_gate,
        grad_values,
        grad_medium,
        grad_long,
        filter_rms,
    )


def solution(mesh):
    spread = P("ctx", "ch")
    shared = P(None, "ch")
    return jax.shard_map(
        body,
        mesh=mesh,
        in_specs=(spread, spread, spread, spread, spread, shared, spread),
        out_specs=(spread, spread, spread, spread, shared, spread, P()),
        check_vma=False,
    )
```

time: 645 us -> 295 us (0.46)
  the two profiles are of different devices: /device:TPU:0 before, /device:TPU:14 now
where the time goes in v1:
time: 295 us; the launch traced here: 291 us
  waiting for transfers between devices  108 us (37%)
  Pallas kernels  99.8 us (34%)
  starting transfers between devices  59.8 us (20%)
  local copies, waits for them, and re-layouts  13.7 us (5%)
  blocking collectives  3.64 us (1%)
  between operations  3.31 us (1%)
    all_to_all x8, starting transfers between devices, swapped(): return lax.all_to_all(array, 'ctx', split_axis=0, concat_axis=0, tiled=True)  53.9 us
    all_to_all x8, waiting for transfers between devices, swapped(): return lax.all_to_all(array, 'ctx', split_axis=0, concat_axis=0, tiled=True)  52.5 us
    ppermute x1, waiting for transfers between devices, body(): prior = lax.ppermute(gated, 'ctx', [(i, i + 1) for i in range(ctx - 1)])  39.5 us
    pallas_call x1, Pallas kernels, body(): pl.pallas_call(functools.partial(mixed_grad_kernel, size), grid=steps, in...  23.4 us
    pallas_call x1, Pallas kernels, body(): pl.pallas_call(functools.partial(ahead_kernel, scale), grid=(own,), in_sp...  20.6 us
    ppermute x1, waiting for transfers between devices, body(): lax.ppermute(grad_mixed, 'ctx', [(i + 1, i) for i in range(ctx - 1)])  16 us
    pallas_call x1, Pallas kernels, body(): pl.pallas_call(functools.partial(gate_grad_kernel, size), grid=steps, in_...  15.5 us
    pallas_call x1, Pallas kernels, body(): pl.pallas_call(functools.partial(forward_kernel, size), grid=steps, in_sp...  15.1 us
  transfers between devices with their start and end apart: 10, of which 6 were waited for; matrix products, arithmetic and copies ran while one was open for 2% of the time, Pallas kernels for 26%

profile of v1, /device:TPU:14, one launch (start us, length us, event | category | flops | bytes accessed | tf_op | source)
XLA Modules:
  0.0 291.0 jit_solution(17530959552356152043)
XLA Ops:
  0.6 1.6 copy.36
  2.2 7.1 %all-to-all-start = ((bf16[16,16,128]{2,1,0:T(8,128)(2,1)}), bf16[16,16,128]{2,1,0:T(8,128)(2,1)S(1)}, u32[]{:S(2)}, u32[]{:S(2)}) async-start(bf16[16,16,128]{2,1,0:T(8,128)(2,1)} %bitcast.2), calls=%async_computation | async-start | bytes 131072 | tf_op jit(solution)/shard_map/all_to_all | solution.py:222
  9.4 1.2 copy-done
  10.6 1.2 copy-done.2
  11.8 1.2 copy-done.4
  13.0 9.5 %shard_map.126 = (bf16[4096,128]{1,0:T(8,128)(2,1)S(1)}, bf16[4096,128]{1,0:T(8,128)(2,1)}) custom-call(bf16[128,4096]{1,0:T(8,128)(2,1)S(1)} %copy-done.2, bf16[128,4096]{1,0:T(8,128)(2,1)S(1)} %copy-done.4, bf16[128,4096]{1,0:T(8,128)(2,1)S(1)} %copy-done, bf16[128,4096]{1,0:T(8,128)(2,1)} %output_ref.1), custom_call_target="tpu_custom_call" | custom-call | tf_op jit(solution)/shard_map/pallas_call | solution.py:212
  22.6 6.9 %all-to-all-start.1 = ((bf16[16,256,128]{2,1,0:T(8,128)(2,1)}), bf16[16,256,128]{2,1,0:T(8,128)(2,1)S(1)}, u32[]{:S(2)}, u32[]{:S(2)}) async-start(bf16[16,256,128]{2,1,0:T(8,128)(2,1)} %bitcast.5), calls=%async_computation.1 | async-start | bytes 2097152 | tf_op jit(solution)/shard_map/all_to_all | solution.py:222
  29.6 23.8 %all-to-all-done.1.inner_ref = bf16[16,256,128]{2,1,0:T(8,128)(2,1)S(1)} async-done(((bf16[16,256,128]{2,1,0:T(8,128)(2,1)}), bf16[16,256,128]{2,1,0:T(8,128)(2,1)S(1)}, u32[]{:S(2)}, u32[]{:S(2)}) %all-to-all-start.1) | async-done | bytes 1048608 | tf_op jit(solution)/shard_map/all_to_all | solution.py:222
  53.3 9.9 %shard_map.127 = bf16[16,256,128]{2,1,0:T(8,128)(2,1)} custom-call(f32[16,1,2048]{2,1,0:T(1,128)S(1)} %bitcast.29, bf16[16,256,128]{2,1,0:T(8,128)(2,1)S(1)} %all-to-all-done.1.inner_ref), custom_call_target="tpu_custom_call" | custom-call | tf_op jit(solution)/shard_map/pallas_call | solution.py:260
  63.2 6.0 %all-to-all-start.2 = ((bf16[16,256,128]{2,1,0:T(8,128)(2,1)}), bf16[16,256,128]{2,1,0:T(8,128)(2,1)}, u32[]{:S(2)}, u32[]{:S(2)}) async-start(bf16[16,256,128]{2,1,0:T(8,128)(2,1)} %shard_map.127), calls=%async_computation.2 | async-start | bytes 2097152 | tf_op jit(solution)/shard_map/all_to_all | solution.py:222
  69.2 3.4 %collective-permute-start = (bf16[4096,128]{1,0:T(8,128)(2,1)S(1)}, bf16[4096,128]{1,0:T(8,128)(2,1)}, u32[]{:S(2)}, u32[]{:S(2)}) collective-permute-start(bf16[4096,128]{1,0:T(8,128)(2,1)S(1)} %get-tuple-element.19.gated_ref), channel_id=1, source_target_pairs={{0,2},{2,4},{4,6},{6,8},{8,10},{10,12},{12,14},{14,16},{16,18},{18... | collective-permute-start | bytes 3145736 | tf_op jit(solution)/shard_map/ppermute | solution.py:226
  73.1 39.5 %collective-permute-done.prior_ref = bf16[4096,128]{1,0:T(8,128)(2,1)} collective-permute-done((bf16[4096,128]{1,0:T(8,128)(2,1)S(1)}, bf16[4096,128]{1,0:T(8,128)(2,1)}, u32[]{:S(2)}, u32[]{:S(2)}) %collective-permute-start) | collective-permute-done | bytes 1048608 | tf_op jit(solution)/shard_map/ppermute | solution.py:226
  112.7 15.1 %shard_map.128 = (f32[4096,128]{1,0:T(8,128)}, bf16[4096,128]{1,0:T(8,128)(2,1)S(1)}) custom-call(f32[256,256]{1,0:T(8,128)S(1)} %maximum_maximum_fusion.base_ref, bf16[4096,128]{1,0:T(8,128)(2,1)} %collective-permute-done.prior_ref, bf16[4096,128]{1,0:T(8,128)(2,1)S(1)} %get-tuple-element.19.gated_ref, bf16[128,4096]{1,0:T(8,128)(2,1)S(1)} %copy-done.6), custom_call_target="tpu_custom_call" | custom-call | tf_op jit(solution)/shard_map/pallas_call | solution.py:240
  127.7 1.0 copy-done.11
  128.7 7.1 %all-to-all-start.3 = ((bf16[16,256,128]{2,1,0:T(8,128)(2,1)}), bf16[16,256,128]{2,1,0:T(8,128)(2,1)S(1)}, u32[]{:S(2)}, u32[]{:S(2)}) async-start(bf16[16,256,128]{2,1,0:T(8,128)(2,1)} %bitcast.31), calls=%async_computation.3 | async-start | bytes 2097152 | tf_op jit(solution)/shard_map/all_to_all | solution.py:222
  135.9 1.2 copy-done.8
  137.1 23.4 %shard_map.129 = (bf16[128,4096]{1,0:T(8,128)(2,1)}, bf16[4096,128]{1,0:T(8,128)(2,1)S(1)}, f32[256,256]{1,0:T(8,128)S(1)}) custom-call(bf16[4096,128]{1,0:T(8,128)(2,1)} %bitcast.6.back_ref, bf16[128,4096]{1,0:T(8,128)(2,1)S(1)} %copy-done.6, f32[4096,128]{1,0:T(8,128)} %get-tuple-element.20.mixed_ref, bf16[4096,128]{1,0:T(8,128)(2,1)S(1)} %copy-done.8, ...), custom_call_target="tpu_custom_call" | custom-call | tf_op jit(solution)/shard_map/pallas_call | solution.py:289
  160.5 1.0 copy-done.9
  162.5 6.9 %all-to-all-start.5 = ((f32[16,16,128]{2,1,0:T(8,128)}), f32[16,16,128]{2,1,0:T(8,128)S(1)}, u32[]{:S(2)}, u32[]{:S(2)}) async-start(f32[16,16,128]{2,1,0:T(8,128)} %bitcast.9), calls=%async_computation.5 | async-start | bytes 262144 | tf_op jit(solution)/shard_map/all_to_all | solution.py:222
  169.4 20.6 %shard_map.131 = (bf16[16,256,128]{2,1,0:T(8,128)(2,1)}, bf16[16,1,2048]{2,1,0:T(2,128)(2,1)S(1)}) custom-call(f32[16,1,2048]{2,1,0:T(1,128)S(1)} %bitcast.30, bf16[16,256,128]{2,1,0:T(8,128)(2,1)S(1)} %all-to-all-done.3.carried_ref, bf16[16,256,128]{2,1,0:T(8,128)(2,1)S(1)} %all-to-all-done.1.inner_ref), custom_call_target="tpu_custom_call" | custom-call | tf_op jit(solution)/shard_map/pallas_call | solution.py:272
  193.5 7.0 %all-to-all-start.6 = ((f32[16,17,128]{2,1,0:T(8,128)}), f32[16,17,128]{2,1,0:T(8,128)S(1)}, u32[]{:S(2)}, u32[]{:S(2)}) async-start(f32[16,17,128]{2,1,0:T(8,128)} %broadcast_in_dim.10), calls=%async_computation.6 | async-start | bytes 393216 | tf_op jit(solution)/shard_map/all_to_all | solution.py:222
  201.5 4.4 %all-to-all-done.6 = f32[16,17,128]{2,1,0:T(8,128)S(1)} async-done(((f32[16,17,128]{2,1,0:T(8,128)}), f32[16,17,128]{2,1,0:T(8,128)S(1)}, u32[]{:S(2)}, u32[]{:S(2)}) %all-to-all-start.6) | async-done | bytes 139296 | tf_op jit(solution)/shard_map/all_to_all | solution.py:222
  205.9 6.1 %all-to-all-start.7 = ((bf16[16,16,128]{2,1,0:T(8,128)(2,1)}), bf16[16,16,128]{2,1,0:T(8,128)(2,1)S(1)}, u32[]{:S(2)}, u32[]{:S(2)}) async-start(bf16[16,16,128]{2,1,0:T(8,128)(2,1)} %copy.38), calls=%async_computation.7 | async-start | bytes 131072 | tf_op jit(solution)/shard_map/all_to_all | solution.py:222
  212.1 4.5 %all-to-all-done.7 = bf16[16,16,128]{2,1,0:T(8,128)(2,1)S(1)} async-done(((bf16[16,16,128]{2,1,0:T(8,128)(2,1)}), bf16[16,16,128]{2,1,0:T(8,128)(2,1)S(1)}, u32[]{:S(2)}, u32[]{:S(2)}) %all-to-all-start.7) | async-done | bytes 65568 | tf_op jit(solution)/shard_map/all_to_all | solution.py:222
  216.6 3.6 %all_to_all.45 = f32[2,1,128]{2,1,0:T(1,128)S(1)} all-to-all(f32[2,1,128]{2,1,0:T(1,128)S(1)} %broadcast_in_dim.11), channel_id=1, replica_groups=mesh['ctx'=16,'ch'=2] {'ch'}, dimensions={0} | all-to-all | bytes 2048 | tf_op jit(solution)/shard_map/all_to_all | solution.py:312
  220.2 6.6 %all-to-all-start.4 = ((bf16[16,256,128]{2,1,0:T(8,128)(2,1)}), bf16[16,256,128]{2,1,0:T(8,128)(2,1)S(1)}, u32[]{:S(2)}, u32[]{:S(2)}) async-start(bf16[16,256,128]{2,1,0:T(8,128)(2,1)} %get-tuple-element.25), calls=%async_computation.4 | async-start | bytes 2097152 | tf_op jit(solution)/shard_map/all_to_all | solution.py:222
  226.8 2.6 collective-permute-start.1
  229.5 1.6 copy.41
  232.8 19.7 %all-to-all-done.4 = bf16[16,256,128]{2,1,0:T(8,128)(2,1)S(1)} async-done(((bf16[16,256,128]{2,1,0:T(8,128)(2,1)}), bf16[16,256,128]{2,1,0:T(8,128)(2,1)S(1)}, u32[]{:S(2)}, u32[]{:S(2)}) %all-to-all-start.4) | async-done | bytes 1048608 | tf_op jit(solution)/shard_map/all_to_all | solution.py:222
  252.6 5.8 %shard_map.132 = bf16[128,4096]{1,0:T(8,128)(2,1)} custom-call(bf16[4096,128]{1,0:T(8,128)(2,1)S(1)} %bitcast.28, bf16[128,4096]{1,0:T(8,128)(2,1)S(1)} %copy-done.1), custom_call_target="tpu_custom_call" | custom-call | tf_op jit(solution)/shard_map/pallas_call | solution.py:325
  258.4 16.0 %collective-permute-done.1.after_ref = bf16[4096,128]{1,0:T(8,128)(2,1)} collective-permute-done((bf16[4096,128]{1,0:T(8,128)(2,1)}, bf16[4096,128]{1,0:T(8,128)(2,1)}, u32[]{:S(2)}, u32[]{:S(2)}) %collective-permute-start.1) | collective-permute-done | bytes 1048608 | tf_op jit(solution)/shard_map/ppermute | solution.py:301
  274.4 15.5 %shard_map.130 = (bf16[128,4096]{1,0:T(8,128)(2,1)}, bf16[128,4096]{1,0:T(8,128)(2,1)}) custom-call(f32[256,256]{1,0:T(8,128)S(1)} %concatenate.9.base_ref, bf16[4096,128]{1,0:T(8,128)(2,1)S(1)} %copy-done.10, bf16[4096,128]{1,0:T(8,128)(2,1)} %collective-permute-done.1.after_ref, bf16[128,4096]{1,0:T(8,128)(2,1)S(1)} %copy-done.3, ...), custom_call_target="tpu_custom_call" | custom-call | tf_op jit(solution)/shard_map/pallas_call | solution.py:316
  (54 shorter events, 6.5 us)
Async XLA Ops:
  2.2 20.4 %all-to-all-start = ((bf16[16,16,128]{2,1,0:T(8,128)(2,1)}), bf16[16,16,128]{2,1,0:T(8,128)(2,1)S(1)}, u32[]{:S(2)}, u32[]{:S(2)}) async-start(bf16[16,16,128]{2,1,0:T(8,128)(2,1)} %bitcast.2), calls=%async_computation | async-start | bytes 131072 | tf_op jit(solution)/shard_map/all_to_all | solution.py:222
  9.3 1.2 copy-start
  10.6 1.2 copy-start.2
  11.8 1.2 copy-start.4
  22.6 90.1 %copy-start.7 = (bf16[4096,128]{1,0:T(8,128)(2,1)}, bf16[4096,128]{1,0:T(8,128)(2,1)S(1)}, u32[]{:S(2)}) copy-start(bf16[4096,128]{1,0:T(8,128)(2,1)S(1)} %get-tuple-element.19.gated_ref) | copy-start | bytes 3145732
  22.6 30.8 %all-to-all-start.1 = ((bf16[16,256,128]{2,1,0:T(8,128)(2,1)}), bf16[16,256,128]{2,1,0:T(8,128)(2,1)S(1)}, u32[]{:S(2)}, u32[]{:S(2)}) async-start(bf16[16,256,128]{2,1,0:T(8,128)(2,1)} %bitcast.5), calls=%async_computation.1 | async-start | bytes 2097152 | tf_op jit(solution)/shard_map/all_to_all | solution.py:222
  53.3 19.2 %copy-start.14 = (bf16[128,256]{1,0:T(8,128)(2,1)S(1)}, bf16[128,256]{1,0:T(8,128)(2,1)}, u32[]{:S(2)}) copy-start(bf16[128,256]{1,0:T(8,128)(2,1)} %param.12) | copy-start | bytes 196612
  63.2 49.5 %copy-start.6 = (bf16[128,4096]{1,0:T(8,128)(2,1)S(1)}, bf16[128,4096]{1,0:T(8,128)(2,1)}, u32[]{:S(2)}) copy-start(bf16[128,4096]{1,0:T(8,128)(2,1)} %second_ref.3) | copy-start | bytes 3145732
  63.2 65.5 %all-to-all-start.2 = ((bf16[16,256,128]{2,1,0:T(8,128)(2,1)}), bf16[16,256,128]{2,1,0:T(8,128)(2,1)}, u32[]{:S(2)}, u32[]{:S(2)}) async-start(bf16[16,256,128]{2,1,0:T(8,128)(2,1)} %shard_map.127), calls=%async_computation.2 | async-start | bytes 2097152 | tf_op jit(solution)/shard_map/all_to_all | solution.py:222
  69.2 43.5 %collective-permute-start = (bf16[4096,128]{1,0:T(8,128)(2,1)S(1)}, bf16[4096,128]{1,0:T(8,128)(2,1)}, u32[]{:S(2)}, u32[]{:S(2)}) collective-permute-start(bf16[4096,128]{1,0:T(8,128)(2,1)S(1)} %get-tuple-element.19.gated_ref), channel_id=1, source_target_pairs={{0,2},{2,4},{4,6},{6,8},{8,10},{10,12},{12,14},{14,16},{16,18},{18... | collective-permute-start | bytes 3145736 | tf_op jit(solution)/shard_map/ppermute | solution.py:226
  127.7 1.0 copy-start.11
  128.7 33.8 %all-to-all-start.3 = ((bf16[16,256,128]{2,1,0:T(8,128)(2,1)}), bf16[16,256,128]{2,1,0:T(8,128)(2,1)S(1)}, u32[]{:S(2)}, u32[]{:S(2)}) async-start(bf16[16,256,128]{2,1,0:T(8,128)(2,1)} %bitcast.31), calls=%async_computation.3 | async-start | bytes 2097152 | tf_op jit(solution)/shard_map/all_to_all | solution.py:222
  135.9 1.2 copy-start.8
  160.5 1.0 copy-start.9
  162.5 28.4 %all-to-all-start.5 = ((f32[16,16,128]{2,1,0:T(8,128)}), f32[16,16,128]{2,1,0:T(8,128)S(1)}, u32[]{:S(2)}, u32[]{:S(2)}) async-start(f32[16,16,128]{2,1,0:T(8,128)} %bitcast.9), calls=%async_computation.5 | async-start | bytes 262144 | tf_op jit(solution)/shard_map/all_to_all | solution.py:222
  193.5 59.1 %copy-start.1 = (bf16[128,4096]{1,0:T(8,128)(2,1)S(1)}, bf16[128,4096]{1,0:T(8,128)(2,1)}, u32[]{:S(2)}) copy-start(bf16[128,4096]{1,0:T(8,128)(2,1)} %cotangent_ref.3) | copy-start | bytes 3145732
  193.5 12.5 %all-to-all-start.6 = ((f32[16,17,128]{2,1,0:T(8,128)}), f32[16,17,128]{2,1,0:T(8,128)S(1)}, u32[]{:S(2)}, u32[]{:S(2)}) async-start(f32[16,17,128]{2,1,0:T(8,128)} %broadcast_in_dim.10), calls=%async_computation.6 | async-start | bytes 393216 | tf_op jit(solution)/shard_map/all_to_all | solution.py:222
  205.9 14.3 %copy-start.12 = (f32[16,17,128]{2,1,0:T(8,128)}, f32[16,17,128]{2,1,0:T(8,128)S(1)}, u32[]{:S(2)}) copy-start(f32[16,17,128]{2,1,0:T(8,128)S(1)} %all-to-all-done.6) | copy-start | bytes 417796
  205.9 10.7 %all-to-all-start.7 = ((bf16[16,16,128]{2,1,0:T(8,128)(2,1)}), bf16[16,16,128]{2,1,0:T(8,128)(2,1)S(1)}, u32[]{:S(2)}, u32[]{:S(2)}) async-start(bf16[16,16,128]{2,1,0:T(8,128)(2,1)} %copy.38), calls=%async_computation.7 | async-start | bytes 131072 | tf_op jit(solution)/shard_map/all_to_all | solution.py:222
  216.6 3.7 %copy-start.13 = (bf16[16,16,128]{2,1,0:T(8,128)(2,1)}, bf16[16,16,128]{2,1,0:T(8,128)(2,1)S(1)}, u32[]{:S(2)}) copy-start(bf16[16,16,128]{2,1,0:T(8,128)(2,1)S(1)} %all-to-all-done.7) | copy-start | bytes 196612
  220.2 32.3 %all-to-all-start.4 = ((bf16[16,256,128]{2,1,0:T(8,128)(2,1)}), bf16[16,256,128]{2,1,0:T(8,128)(2,1)S(1)}, u32[]{:S(2)}, u32[]{:S(2)}) async-start(bf16[16,256,128]{2,1,0:T(8,128)(2,1)} %get-tuple-element.25), calls=%async_computation.4 | async-start | bytes 2097152 | tf_op jit(solution)/shard_map/all_to_all | solution.py:222
  226.8 47.6 %copy-start.3 = (bf16[128,4096]{1,0:T(8,128)(2,1)S(1)}, bf16[128,4096]{1,0:T(8,128)(2,1)}, u32[]{:S(2)}) copy-start(bf16[128,4096]{1,0:T(8,128)(2,1)} %first_ref.3) | copy-start | bytes 3145732
  226.8 47.6 %collective-permute-start.1 = (bf16[4096,128]{1,0:T(8,128)(2,1)}, bf16[4096,128]{1,0:T(8,128)(2,1)}, u32[]{:S(2)}, u32[]{:S(2)}) collective-permute-start(bf16[4096,128]{1,0:T(8,128)(2,1)} %copy-done.9), channel_id=1, source_target_pairs={{2,0},{4,2},{6,4},{8,6},{10,8},{12,10},{14,12},{16,14},{18,16},{20... | collective-permute-start | bytes 3145736 | tf_op jit(solution)/shard_map/ppermute | solution.py:301
  252.6 21.9 %copy-start.5 = (bf16[128,4096]{1,0:T(8,128)(2,1)S(1)}, bf16[128,4096]{1,0:T(8,128)(2,1)}, u32[]{:S(2)}) copy-start(bf16[128,4096]{1,0:T(8,128)(2,1)} %values_ref.3) | copy-start | bytes 3145732
  252.6 21.9 %copy-start.10 = (bf16[4096,128]{1,0:T(8,128)(2,1)S(1)}, bf16[4096,128]{1,0:T(8,128)(2,1)}, u32[]{:S(2)}) copy-start(bf16[4096,128]{1,0:T(8,128)(2,1)} %copy-done.9) | copy-start | bytes 3145732

commit v2 on v1

--- a/solution.py
+++ b/solution.py
@@ -11,11 +11,18 @@
 wide = jnp.float32
 narrow = jnp.bfloat16
 params = pltpu.CompilerParams(vmem_limit_bytes=48 * 1024 * 1024)
+peak = 1.1e9
+
+
+def cost(micros, channels):
+    scaled = int(micros * peak * channels / 4096)
+    return pl.CostEstimate(flops=scaled, bytes_accessed=0, transcendentals=0)
 
 
 def rolled_rows(row, rows):
     width = row.shape[1]
     base = pltpu.roll(jnp.broadcast_to(row, (16, width)), 0, 1, stride=1, stride_axis=0)
+    base = base.astype(narrow)
     parts = [base]
     for number in range(1, rows // 16):
         parts.append(pltpu.roll(base, 16 * number, 1))
@@ -33,11 +40,16 @@
     return total
 
 
-def prep_kernel(first_ref, values_ref, cotangent_ref, output_ref, gated_ref, inner_ref):
+def gated_kernel(first_ref, values_ref, gated_ref):
     gated = first_ref[...].astype(wide) * values_ref[...].astype(wide)
     gated_ref[...] = gated.astype(narrow).T
+
+
+def inner_kernel(cotangent_ref, output_ref, filter_ref, slab_ref):
     inner = cotangent_ref[...].astype(wide) * output_ref[...].astype(wide)
-    inner_ref[...] = inner.astype(narrow).T
+    width = inner.shape[1]
+    slab_ref[0, :width] = inner.astype(narrow).T
+    slab_ref[0, width:] = filter_ref[0]
 
 
 def forward_kernel(size, base_ref, prior_ref, gated_ref, second_ref, mixed_ref, carried_ref):
@@ -209,21 +221,48 @@
     base_block = pl.BlockSpec((step_groups, 2 * tokens), lambda i: (i, 0))
     channel_shape = (channels, tokens)
 
-    gated, inner = pl.pallas_call(
-        prep_kernel,
+    gated = pl.pallas_call(
+        gated_kernel,
         grid=steps,
-        in_specs=[by_token] * 4,
-        out_specs=[by_channel] * 2,
-        out_shape=[shape_of(channel_shape, narrow)] * 2,
-        compiler_params=params,
-    )(first_gate, values, cotangent, output_gate)
+        in_specs=[by_token] * 2,
+        out_specs=by_channel,
+        out_shape=shape_of(channel_shape, narrow),
+        compiler_params=params,
+        cost_estimate=cost(5, channels),
+    )(first_gate, values)
+    prior = lax.ppermute(gated, "ctx", [(i, i + 1) for i in range(ctx - 1)])
 
     def swapped(array):
         return lax.all_to_all(array, "ctx", split_axis=0, concat_axis=0, tiled=True)
 
-    filters = swapped(long_filter.T.reshape(ctx, own, tokens))
-    inner_all = swapped(inner.reshape(ctx, own * size, tokens))
-    prior = lax.ppermute(gated, "ctx", [(i, i + 1) for i in range(ctx - 1)])
+    slab_width = own * size
+    slab_token = pl.BlockSpec((tokens, slab_width), lambda i: (0, i))
+    if slab_width % 128:
+        slab = jnp.concatenate(
+            [
+                (cotangent.astype(wide) * output_gate.astype(wide))
+                .astype(narrow)
+                .T.reshape(ctx, slab_width, tokens),
+                long_filter.T.reshape(ctx, own, tokens),
+            ],
+            axis=1,
+        )
+    else:
+        slab = pl.pallas_call(
+            inner_kernel,
+            grid=(ctx,),
+            in_specs=[
+                slab_token,
+                slab_token,
+                pl.BlockSpec((1, own, tokens), lambda i: (i, 0, 0)),
+            ],
+            out_specs=pl.BlockSpec((1, slab_width + own, tokens), lambda i: (i, 0, 0)),
+            out_shape=shape_of((ctx, slab_width + own, tokens), narrow),
+            compiler_params=params,
+            cost_estimate=cost(5, channels),
+        )(cotangent, output_gate, long_filter.T.reshape(ctx, own, tokens))
+    slab, prior = lax.optimization_barrier((slab, prior))
+    slab_all = swapped(slab)
 
     turned = medium_filter.T.astype(wide)
     pad = 2 * tokens - taps
@@ -244,14 +283,16 @@
         out_specs=[by_channel] * 2,
         out_shape=[shape_of(channel_shape, wide), shape_of(channel_shape, narrow)],
         compiler_params=params,
+        cost_estimate=cost(15, channels),
     )(forward_base, prior, gated, second_gate)
-    carried_all = swapped(carried.reshape(ctx, own * size, tokens))
+    carried, slab_all = lax.optimization_barrier((carried, slab_all))
+    carried_all = swapped(carried.reshape(ctx, slab_width, tokens))
 
     length = ctx * tokens
-    filter_rows = filters.transpose(1, 0, 2).reshape(own, 1, length).astype(wide)
+    filter_rows = slab_all[:, slab_width:].transpose(1, 0, 2).reshape(own, 1, length).astype(wide)
     row_block = pl.BlockSpec((1, 1, length), lambda g: (g, 0, 0))
     piece = pl.BlockSpec((ctx, size, tokens), lambda g: (0, g, 0))
-    all_shape = (ctx, own * size, tokens)
+    all_shape = (ctx, slab_width, tokens)
     scratch = [
         pltpu.VMEM((tokens, length), narrow),
         pltpu.VMEM((ctx * size, 2 * tokens), narrow),
@@ -265,7 +306,9 @@
         out_shape=shape_of(all_shape, narrow),
         scratch_shapes=scratch,
         compiler_params=params,
-    )(filter_rows, inner_all)
+        cost_estimate=cost(10, channels),
+    )(filter_rows, slab_all)
+    back_all, carried_all = lax.optimization_barrier((back_all, carried_all))
     back = swapped(back_all).reshape(channel_shape)
 
     scale = 1.0 / math.sqrt(length * size)
@@ -281,10 +324,10 @@
             pltpu.VMEM((tokens, length), wide),
         ],
         compiler_params=params,
-    )(filter_rows, carried_all, inner_all)
+        cost_estimate=cost(23, channels),
+    )(filter_rows, carried_all, slab_all)
+    ahead_all, long_rows, back = lax.optimization_barrier((ahead_all, long_rows, back))
     ahead = swapped(ahead_all).reshape(channel_shape)
-    long_pieces = long_rows.reshape(own, ctx, tokens).transpose(1, 0, 2)
-    grad_long = swapped(long_pieces).reshape(groups, tokens).T
 
     grad_second, grad_mixed, sums = pl.pallas_call(
         functools.partial(mixed_grad_kernel, size),
@@ -297,20 +340,43 @@
             shape_of((groups, 2 * tokens), wide),
         ],
         compiler_params=params,
+        cost_estimate=cost(20, channels),
     )(back, second_gate, mixed, gated, prior)
+    ahead, grad_mixed, sums = lax.optimization_barrier((ahead, grad_mixed, sums))
     after = lax.ppermute(grad_mixed, "ctx", [(i + 1, i) for i in range(ctx - 1)])
 
     terms = sums[:, tokens + 1 - taps : tokens + 1][:, ::-1] * scale
-    medium_own = jnp.sum(swapped(terms.reshape(ctx, own, taps)), axis=0)
+    long_pieces = long_rows.reshape(own, ctx, tokens).transpose(1, 0, 2).astype(wide)
+    filter_terms = swapped(
+        jnp.concatenate([terms.reshape(ctx, own, taps), long_pieces], axis=2)
+    )
+    grad_long = filter_terms[:, :, taps:].reshape(groups, tokens).T.astype(narrow)
+    medium_own = jnp.sum(filter_terms[:, :, :taps], axis=0)
     squares = jnp.sum(jnp.square(medium_own)) + jnp.sum(jnp.square(long_rows.astype(wide)))
     package = jnp.concatenate([medium_own, jnp.full((1, taps), squares, wide)], axis=0)
-    gathered = swapped(jnp.broadcast_to(package[None], (ctx, own + 1, taps)))
-    grad_medium = gathered[:, :own].reshape(groups, taps).T
+    grad_output_gate = pl.pallas_call(
+        output_grad_kernel,
+        grid=steps,
+        in_specs=[by_channel, by_token],
+        out_specs=by_token,
+        out_shape=shape_of((tokens, channels), narrow),
+        compiler_params=params,
+        cost_estimate=cost(6, channels),
+    )(ahead, cotangent)
+    package, after, grad_output_gate = lax.optimization_barrier(
+        (package, after, grad_output_gate)
+    )
     ch = lax.axis_size("ch")
-    side = jnp.broadcast_to(jnp.sum(gathered[:, own], axis=0)[None, None], (ch, 1, taps))
-    total = jnp.sum(
-        lax.all_to_all(side, "ch", split_axis=0, concat_axis=0, tiled=True), axis=0
-    )[0, 0]
+    gathered = lax.all_to_all(
+        jnp.broadcast_to(package[None], (ctx * ch, own + 1, taps)),
+        ("ctx", "ch"),
+        split_axis=0,
+        concat_axis=0,
+        tiled=True,
+    ).reshape(ctx, ch, own + 1, taps)
+    mine = lax.dynamic_index_in_dim(gathered, lax.axis_index("ch"), 1, keepdims=False)
+    grad_medium = mine[:, :own].reshape(groups, taps).T
+    total = jnp.sum(gathered[:, :, own, 0])
     filter_rms = jnp.sqrt(total / ((length + taps) * groups * ch))
 
     grad_first, grad_values = pl.pallas_call(
@@ -321,15 +387,8 @@
         out_shape=[shape_of((tokens, channels), narrow)] * 2,
         scratch_shapes=[pltpu.VMEM((width, tokens), wide)],
         compiler_params=params,
+        cost_estimate=cost(15, channels),
     )(reverse_base, grad_mixed, after, first_gate, values)
-    grad_output_gate = pl.pallas_call(
-        output_grad_kernel,
-        grid=steps,
-        in_specs=[by_channel, by_token],
-        out_specs=by_token,
-        out_shape=shape_of((tokens, channels), narrow),
-        compiler_params=params,
-    )(ahead, cotangent)
     return (
         grad_first,
         grad_second,

time: 295 us -> 226 us (0.77)
  the two profiles are of different devices: /device:TPU:14 before, /device:TPU:0 now
where the time goes in v2:
time: 226 us; the launch traced here: 224 us
  Pallas kernels  97.7 us (43%)
  waiting for transfers between devices  56.8 us (25%)
  starting transfers between devices  47 us (21%)
  local copies, waits for them, and re-layouts  14 us (6%)
  between operations  4.07 us (2%)
  other arithmetic  4.06 us (2%)
    all_to_all x5, waiting for transfers between devices, swapped(): return lax.all_to_all(array, 'ctx', split_axis=0, concat_axis=0, tiled=True)  41 us
    all_to_all x5, starting transfers between devices, swapped(): return lax.all_to_all(array, 'ctx', split_axis=0, concat_axis=0, tiled=True)  34.9 us
    pallas_call x1, Pallas kernels, body(): pl.pallas_call(functools.partial(mixed_grad_kernel, size), grid=steps, in...  23.5 us
    pallas_call x1, Pallas kernels, body(): pl.pallas_call(functools.partial(ahead_kernel, scale), grid=(own,), in_sp...  19.4 us
    ppermute x1, waiting for transfers between devices, body(): prior = lax.ppermute(gated, 'ctx', [(i, i + 1) for i in range(ctx - 1)])  15.7 us
    pallas_call x1, Pallas kernels, body(): pl.pallas_call(functools.partial(gate_grad_kernel, size), grid=steps, in_...  14.5 us
    pallas_call x1, Pallas kernels, body(): pl.pallas_call(functools.partial(forward_kernel, size), grid=steps, in_sp...  14 us
    unnamed x35, local copies, waits for them, and re-layouts  9.58 us
  transfers between devices with their start and end apart: 8, of which 5 were waited for; matrix products, arithmetic and copies ran while one was open for 3% of the time, Pallas kernels for 41%

profile of v2, /device:TPU:0, one launch (start us, length us, event | category | flops | bytes accessed | tf_op | source)
XLA Modules:
  0.0 223.6 jit_solution(8340542140852327329)
XLA Ops:
  0.7 1.4 copy-done.8
  2.0 1.2 copy-done.10
  3.3 5.9 %shard_map.127.gated_ref = bf16[4096,128]{1,0:T(8,128)(2,1)} custom-call(bf16[128,4096]{1,0:T(8,128)(2,1)S(1)} %copy-done.8, bf16[128,4096]{1,0:T(8,128)(2,1)S(1)} %copy-done.10), custom_call_target="tpu_custom_call" | custom-call | flops 5500000256 | tf_op jit(solution)/shard_map/pallas_call | solution.py:224
  9.1 5.8 %collective-permute-start = (bf16[4096,128]{1,0:T(8,128)(2,1)}, bf16[4096,128]{1,0:T(8,128)(2,1)}, u32[]{:S(2)}, u32[]{:S(2)}) collective-permute-start(bf16[4096,128]{1,0:T(8,128)(2,1)} %shard_map.127.gated_ref), channel_id=1, source_target_pairs={{0,2},{2,4},{4,6},{6,8},{8,10},{10,12},{12,14},{14,16},{16,18},{18... | collective-permute-start | bytes 3145736 | tf_op jit(solution)/shard_map/ppermute | solution.py:233
  15.1 5.9 %shard_map.126 = bf16[16,272,128]{2,1,0:T(8,128)(2,1)} custom-call(bf16[128,4096]{1,0:T(8,128)(2,1)S(1)} %copy-done.6, bf16[128,4096]{1,0:T(8,128)(2,1)S(1)} %copy-done.3, bf16[16,16,128]{2,1,0:T(8,128)(2,1)S(1)} %bitcast.28), custom_call_target="tpu_custom_call" | custom-call | flops 5500000256 | tf_op jit(solution)/shard_map/pallas_call | solution.py:251
  21.0 15.7 %collective-permute-done.prior_ref = bf16[4096,128]{1,0:T(8,128)(2,1)} collective-permute-done((bf16[4096,128]{1,0:T(8,128)(2,1)}, bf16[4096,128]{1,0:T(8,128)(2,1)}, u32[]{:S(2)}, u32[]{:S(2)}) %collective-permute-start) | collective-permute-done | bytes 1048608 | tf_op jit(solution)/shard_map/ppermute | solution.py:233
  36.7 7.9 %all-to-all-start = ((bf16[16,272,128]{2,1,0:T(8,128)(2,1)}), bf16[16,272,128]{2,1,0:T(8,128)(2,1)S(1)}, u32[]{:S(2)}, u32[]{:S(2)}) async-start(bf16[16,272,128]{2,1,0:T(8,128)(2,1)} %shard_map.126), calls=%async_computation | async-start | bytes 2228224 | tf_op jit(solution)/shard_map/all_to_all | solution.py:236
  45.1 14.0 %shard_map.128 = (f32[4096,128]{1,0:T(8,128)}, bf16[4096,128]{1,0:T(8,128)(2,1)}) custom-call(f32[256,256]{1,0:T(8,128)S(1)} %maximum_maximum_fusion.base_ref, bf16[4096,128]{1,0:T(8,128)(2,1)} %collective-permute-done.prior_ref, bf16[4096,128]{1,0:T(8,128)(2,1)} %shard_map.127.gated_ref, bf16[128,4096]{1,0:T(8,128)(2,1)S(1)} %copy-done.4), custom_call_target="tpu_custom_call" | custom-call | flops 16499999744 | tf_op jit(solution)/shard_map/pallas_call | solution.py:279
  59.1 10.3 %all-to-all-done.inner_ref = bf16[16,272,128]{2,1,0:T(8,128)(2,1)S(1)} async-done(((bf16[16,272,128]{2,1,0:T(8,128)(2,1)}), bf16[16,272,128]{2,1,0:T(8,128)(2,1)S(1)}, u32[]{:S(2)}, u32[]{:S(2)}) %all-to-all-start) | async-done | bytes 1114144 | tf_op jit(solution)/shard_map/all_to_all | solution.py:236
  69.4 5.9 %all-to-all-start.1 = ((bf16[16,256,128]{2,1,0:T(8,128)(2,1)}), bf16[16,256,128]{2,1,0:T(8,128)(2,1)S(1)}, u32[]{:S(2)}, u32[]{:S(2)}) async-start(bf16[16,256,128]{2,1,0:T(8,128)(2,1)} %bitcast.5), calls=%async_computation.1 | async-start | bytes 2097152 | tf_op jit(solution)/shard_map/all_to_all | solution.py:236
  76.2 8.7 %shard_map.129 = bf16[16,256,128]{2,1,0:T(8,128)(2,1)S(1)} custom-call(f32[16,1,2048]{2,1,0:T(1,128)S(1)} %bitcast.26, bf16[16,272,128]{2,1,0:T(8,128)(2,1)S(1)} %all-to-all-done.inner_ref), custom_call_target="tpu_custom_call" | custom-call | flops 11000000512 | tf_op jit(solution)/shard_map/pallas_call | solution.py:301
  84.9 1.0 copy-done.1
  85.8 12.4 %all-to-all-done.1.carried_ref = bf16[16,256,128]{2,1,0:T(8,128)(2,1)S(1)} async-done(((bf16[16,256,128]{2,1,0:T(8,128)(2,1)}), bf16[16,256,128]{2,1,0:T(8,128)(2,1)S(1)}, u32[]{:S(2)}, u32[]{:S(2)}) %all-to-all-start.1) | async-done | bytes 1048608 | tf_op jit(solution)/shard_map/all_to_all | solution.py:236
  98.2 6.0 %all-to-all-start.2 = ((bf16[16,256,128]{2,1,0:T(8,128)(2,1)}), bf16[16,256,128]{2,1,0:T(8,128)(2,1)S(1)}, u32[]{:S(2)}, u32[]{:S(2)}) async-start(bf16[16,256,128]{2,1,0:T(8,128)(2,1)} %copy-done.1), calls=%async_computation.2 | async-start | bytes 2097152 | tf_op jit(solution)/shard_map/all_to_all | solution.py:236
  104.3 19.4 %shard_map.130 = (bf16[16,256,128]{2,1,0:T(8,128)(2,1)S(1)}, bf16[16,1,2048]{2,1,0:T(2,128)(2,1)S(1)}) custom-call(f32[16,1,2048]{2,1,0:T(1,128)S(1)} %bitcast.27, bf16[16,256,128]{2,1,0:T(8,128)(2,1)S(1)} %all-to-all-done.1.carried_ref, bf16[16,272,128]{2,1,0:T(8,128)(2,1)S(1)} %all-to-all-done.inner_ref), custom_call_target="tpu_custom_call" | custom-call | flops 25300000768 | tf_op jit(solution)/shard_map/pallas_call | solution.py:315
  123.7 1.0 copy-done
  124.7 2.4 %all-to-all-done.2 = bf16[16,256,128]{2,1,0:T(8,128)(2,1)S(1)} async-done(((bf16[16,256,128]{2,1,0:T(8,128)(2,1)}), bf16[16,256,128]{2,1,0:T(8,128)(2,1)S(1)}, u32[]{:S(2)}, u32[]{:S(2)}) %all-to-all-start.2) | async-done | bytes 1048608 | tf_op jit(solution)/shard_map/all_to_all | solution.py:236
  127.3 0.9 multiply_reduce_fusion
  128.1 6.0 %all-to-all-start.3 = ((bf16[16,256,128]{2,1,0:T(8,128)(2,1)}), bf16[16,256,128]{2,1,0:T(8,128)(2,1)S(1)}, u32[]{:S(2)}, u32[]{:S(2)}) async-start(bf16[16,256,128]{2,1,0:T(8,128)(2,1)} %copy-done), calls=%async_computation.3 | async-start | bytes 2097152 | tf_op jit(solution)/shard_map/all_to_all | solution.py:236
  134.2 1.2 copy-done.5
  135.4 23.5 %shard_map.131 = (bf16[128,4096]{1,0:T(8,128)(2,1)}, bf16[4096,128]{1,0:T(8,128)(2,1)S(1)}, f32[256,256]{1,0:T(8,128)S(1)}) custom-call(bf16[4096,128]{1,0:T(8,128)(2,1)S(1)} %bitcast.25, bf16[128,4096]{1,0:T(8,128)(2,1)S(1)} %copy-done.5, f32[4096,128]{1,0:T(8,128)} %get-tuple-element.42.mixed_ref, bf16[4096,128]{1,0:T(8,128)(2,1)} %shard_map.127.gated_ref, ...), custom_call_target="tpu_custom_call" | custom-call | flops 22000001024 | tf_op jit(solution)/shard_map/pallas_call | solution.py:332
  158.9 1.0 copy-done.12
  159.9 1.4 collective-permute-start.1
  162.4 9.1 %all-to-all-start.4 = ((f32[16,16,256]{2,1,0:T(8,128)}), f32[16,16,256]{2,1,0:T(8,128)}, u32[]{:S(2)}, u32[]{:S(2)}) async-start(f32[16,16,256]{2,1,0:T(8,128)} %pad_maximum_fusion), calls=%async_computation.4 | async-start | bytes 524288 | tf_op jit(solution)/shard_map/all_to_all | solution.py:236
  171.5 5.8 %shard_map.132 = bf16[128,4096]{1,0:T(8,128)(2,1)} custom-call(bf16[4096,128]{1,0:T(8,128)(2,1)S(1)} %bitcast.24, bf16[128,4096]{1,0:T(8,128)(2,1)S(1)} %copy-done.7), custom_call_target="tpu_custom_call" | custom-call | flops 6600000000 | tf_op jit(solution)/shard_map/pallas_call | solution.py:357
  177.4 15.9 %all-to-all-done.4 = f32[16,16,256]{2,1,0:T(8,128)} async-done(((f32[16,16,256]{2,1,0:T(8,128)}), f32[16,16,256]{2,1,0:T(8,128)}, u32[]{:S(2)}, u32[]{:S(2)}) %all-to-all-start.4) | async-done | bytes 262176 | tf_op jit(solution)/shard_map/all_to_all | solution.py:236
  193.2 0.9 slice_reduce_fusion
  196.1 0.9 slice.33
  198.5 4.8 %all-to-all-start.5 = ((f32[32,17,128]{2,1,0:T(8,128)}), f32[32,17,128]{2,1,0:T(8,128)}, u32[]{:S(2)}, u32[]{:S(2)}) async-start(f32[32,17,128]{2,1,0:T(8,128)} %broadcast_in_dim.16), calls=%async_computation.5 | async-start | bytes 786432 | tf_op jit(solution)/shard_map/all_to_all | solution.py:370
  203.4 1.2 copy-done.13
  204.6 14.5 %shard_map.133 = (bf16[128,4096]{1,0:T(8,128)(2,1)}, bf16[128,4096]{1,0:T(8,128)(2,1)}) custom-call(f32[256,256]{1,0:T(8,128)S(1)} %copy-done.2, bf16[4096,128]{1,0:T(8,128)(2,1)S(1)} %copy-done.13, bf16[4096,128]{1,0:T(8,128)(2,1)} %collective-permute-done.1.after_ref, bf16[128,4096]{1,0:T(8,128)(2,1)S(1)} %copy-done.9, bf16[128,4096]{1,0:T(8,128)(2,1)S(1)} %copy-done.11), custom_call_target="tpu_custom_call" | custom-call | flops 16499999744 | tf_op jit(solution)/shard_map/pallas_call | solution.py:382
  219.1 1.1 copy.41
  (54 shorter events, 6.4 us)
Async XLA Ops:
  0.6 14.4 %copy-start.6 = (bf16[128,4096]{1,0:T(8,128)(2,1)S(1)}, bf16[128,4096]{1,0:T(8,128)(2,1)}, u32[]{:S(2)}) copy-start(bf16[128,4096]{1,0:T(8,128)(2,1)} %cotangent_ref.3) | copy-start | bytes 3145732
  0.6 14.4 %copy-start.3 = (bf16[128,4096]{1,0:T(8,128)(2,1)S(1)}, bf16[128,4096]{1,0:T(8,128)(2,1)}, u32[]{:S(2)}) copy-start(bf16[128,4096]{1,0:T(8,128)(2,1)} %output_ref.1) | copy-start | bytes 3145732
  0.7 1.4 copy-start.8
  2.0 1.2 copy-start.10
  3.3 11.7 %copy-start.14 = (bf16[128,256]{1,0:T(8,128)(2,1)S(1)}, bf16[128,256]{1,0:T(8,128)(2,1)}, u32[]{:S(2)}) copy-start(bf16[128,256]{1,0:T(8,128)(2,1)} %param.13) | copy-start | bytes 196612
  9.1 27.6 %collective-permute-start = (bf16[4096,128]{1,0:T(8,128)(2,1)}, bf16[4096,128]{1,0:T(8,128)(2,1)}, u32[]{:S(2)}, u32[]{:S(2)}) collective-permute-start(bf16[4096,128]{1,0:T(8,128)(2,1)} %shard_map.127.gated_ref), channel_id=1, source_target_pairs={{0,2},{2,4},{4,6},{6,8},{8,10},{10,12},{12,14},{14,16},{16,18},{18... | collective-permute-start | bytes 3145736 | tf_op jit(solution)/shard_map/ppermute | solution.py:233
  21.0 23.6 %copy-start.15 = (bf16[128,256]{1,0:T(8,128)(2,1)S(1)}, bf16[128,256]{1,0:T(8,128)(2,1)}, u32[]{:S(2)}) copy-start(bf16[128,256]{1,0:T(8,128)(2,1)} %param.12) | copy-start | bytes 196612
  21.0 24.2 %copy-start.4 = (bf16[128,4096]{1,0:T(8,128)(2,1)S(1)}, bf16[128,4096]{1,0:T(8,128)(2,1)}, u32[]{:S(2)}) copy-start(bf16[128,4096]{1,0:T(8,128)(2,1)} %second_ref.3) | copy-start | bytes 3145732
  36.7 32.7 %all-to-all-start = ((bf16[16,272,128]{2,1,0:T(8,128)(2,1)}), bf16[16,272,128]{2,1,0:T(8,128)(2,1)S(1)}, u32[]{:S(2)}, u32[]{:S(2)}) async-start(bf16[16,272,128]{2,1,0:T(8,128)(2,1)} %shard_map.126), calls=%async_computation | async-start | bytes 2228224 | tf_op jit(solution)/shard_map/all_to_all | solution.py:236
  69.4 28.8 %all-to-all-start.1 = ((bf16[16,256,128]{2,1,0:T(8,128)(2,1)}), bf16[16,256,128]{2,1,0:T(8,128)(2,1)S(1)}, u32[]{:S(2)}, u32[]{:S(2)}) async-start(bf16[16,256,128]{2,1,0:T(8,128)(2,1)} %bitcast.5), calls=%async_computation.1 | async-start | bytes 2097152 | tf_op jit(solution)/shard_map/all_to_all | solution.py:236
  84.9 1.0 copy-start.1
  98.2 28.9 %all-to-all-start.2 = ((bf16[16,256,128]{2,1,0:T(8,128)(2,1)}), bf16[16,256,128]{2,1,0:T(8,128)(2,1)S(1)}, u32[]{:S(2)}, u32[]{:S(2)}) async-start(bf16[16,256,128]{2,1,0:T(8,128)(2,1)} %copy-done.1), calls=%async_computation.2 | async-start | bytes 2097152 | tf_op jit(solution)/shard_map/all_to_all | solution.py:236
  123.7 1.0 copy-start
  128.1 31.8 %all-to-all-start.3 = ((bf16[16,256,128]{2,1,0:T(8,128)(2,1)}), bf16[16,256,128]{2,1,0:T(8,128)(2,1)S(1)}, u32[]{:S(2)}, u32[]{:S(2)}) async-start(bf16[16,256,128]{2,1,0:T(8,128)(2,1)} %copy-done), calls=%async_computation.3 | async-start | bytes 2097152 | tf_op jit(solution)/shard_map/all_to_all | solution.py:236
  134.2 1.2 copy-start.5
  158.9 1.0 copy-start.12
  159.9 11.6 %copy-start.7 = (bf16[128,4096]{1,0:T(8,128)(2,1)S(1)}, bf16[128,4096]{1,0:T(8,128)(2,1)}, u32[]{:S(2)}) copy-start(bf16[128,4096]{1,0:T(8,128)(2,1)} %cotangent_ref.3) | copy-start | bytes 3145732
  159.9 37.8 %collective-permute-start.1 = (bf16[4096,128]{1,0:T(8,128)(2,1)}, bf16[4096,128]{1,0:T(8,128)(2,1)}, u32[]{:S(2)}, u32[]{:S(2)}) collective-permute-start(bf16[4096,128]{1,0:T(8,128)(2,1)} %copy-done.12), channel_id=1, source_target_pairs={{2,0},{4,2},{6,4},{8,6},{10,8},{12,10},{14,12},{16,14},{18,16},{20... | collective-permute-start | bytes 3145736 | tf_op jit(solution)/shard_map/ppermute | solution.py:346
  162.4 30.9 %all-to-all-start.4 = ((f32[16,16,256]{2,1,0:T(8,128)}), f32[16,16,256]{2,1,0:T(8,128)}, u32[]{:S(2)}, u32[]{:S(2)}) async-start(f32[16,16,256]{2,1,0:T(8,128)} %pad_maximum_fusion), calls=%async_computation.4 | async-start | bytes 524288 | tf_op jit(solution)/shard_map/all_to_all | solution.py:236
  171.5 31.8 %copy-start.11 = (bf16[128,4096]{1,0:T(8,128)(2,1)S(1)}, bf16[128,4096]{1,0:T(8,128)(2,1)}, u32[]{:S(2)}) copy-start(bf16[128,4096]{1,0:T(8,128)(2,1)} %values_ref.3) | copy-start | bytes 3145732
  177.4 26.0 %copy-start.2 = (f32[256,256]{1,0:T(8,128)S(1)}, f32[256,256]{1,0:T(8,128)}, u32[]{:S(2)}) copy-start(f32[256,256]{1,0:T(8,128)} %concatenate.12.base_ref) | copy-start | bytes 786436
  177.4 26.0 %copy-start.9 = (bf16[128,4096]{1,0:T(8,128)(2,1)S(1)}, bf16[128,4096]{1,0:T(8,128)(2,1)}, u32[]{:S(2)}) copy-start(bf16[128,4096]{1,0:T(8,128)(2,1)} %first_ref.3) | copy-start | bytes 3145732
  198.5 20.6 %all-to-all-start.5 = ((f32[32,17,128]{2,1,0:T(8,128)}), f32[32,17,128]{2,1,0:T(8,128)}, u32[]{:S(2)}, u32[]{:S(2)}) async-start(f32[32,17,128]{2,1,0:T(8,128)} %broadcast_in_dim.16), calls=%async_computation.5 | async-start | bytes 786432 | tf_op jit(solution)/shard_map/all_to_all | solution.py:370
  203.4 1.2 copy-start.13

commit v3 on v2

--- a/solution.py
+++ b/solution.py
@@ -40,6 +40,12 @@
     return total
 
 
+def lower_mask(tokens):
+    rows = lax.broadcasted_iota(jnp.int32, (tokens, tokens), 0)
+    lanes = lax.broadcasted_iota(jnp.int32, (tokens, tokens), 1)
+    return rows, lanes
+
+
 def gated_kernel(first_ref, values_ref, gated_ref):
     gated = first_ref[...].astype(wide) * values_ref[...].astype(wide)
     gated_ref[...] = gated.astype(narrow).T
@@ -54,10 +60,15 @@
 
 def forward_kernel(size, base_ref, prior_ref, gated_ref, second_ref, mixed_ref, carried_ref):
     gate = second_ref[...].T
+    tokens = gated_ref.shape[1]
+    row_ids, lane_ids = lower_mask(tokens)
+    keep = jnp.where(lane_ids <= row_ids, 1.0, 0.0).astype(narrow)
     for number in range(base_ref.shape[0]):
         rows = slice(number * size, (number + 1) * size)
         extended = jnp.concatenate([prior_ref[rows], gated_ref[rows]], axis=1)
-        band = rolled_rows(base_ref[number : number + 1, :], gated_ref.shape[1])
+        whole = rolled_rows(base_ref[number : number + 1, :], tokens)
+        near = whole * keep
+        band = jnp.concatenate([whole - near, near], axis=1)
         mixed = lax.dot_general(
             extended, band, (((1,), (1,)), ((), ())), preferred_element_type=wide
         )
@@ -155,14 +166,19 @@
     long_ref[0] = (diagonal_sums(lagged_ref[...]) * scale).astype(narrow)
 
 
-def mixed_grad_kernel(
-    size, back_ref, second_ref, mixed_ref, gated_ref, prior_ref, grad_second_ref, grad_mixed_ref, sums_ref
-):
-    tokens = second_ref.shape[0]
+def mixed_grad_kernel(back_ref, second_ref, mixed_ref, grad_second_ref, grad_mixed_ref, token_ref):
     back = back_ref[...].astype(wide)
     grad_second_ref[...] = (back * mixed_ref[...]).T.astype(narrow)
     grad_mixed = (back_ref[...].T.astype(wide) * second_ref[...].astype(wide)).astype(narrow)
+    token_ref[...] = grad_mixed
     grad_mixed_ref[...] = grad_mixed.T
+
+
+def medium_kernel(size, grad_mixed_ref, gated_ref, prior_ref, sums_ref):
+    tokens = grad_mixed_ref.shape[0]
+    row_ids, lane_ids = lower_mask(tokens)
+    keep = lane_ids <= row_ids
+    grad_mixed = grad_mixed_ref[...]
     per = 128 // size
     for number in range(sums_ref.shape[0]):
         rows = slice(number * size, (number + 1) * size)
@@ -179,16 +195,22 @@
         product = jnp.dot(
             grad_mixed[:, start : start + 128], weights, preferred_element_type=wide
         )
-        sums_ref[number : number + 1, :] = diagonal_sums(product)
+        folded = jnp.where(keep, product[:, tokens:], product[:, :tokens])
+        sums_ref[number : number + 1, :] = diagonal_sums(folded)
 
 
 def gate_grad_kernel(
     size, base_ref, grad_mixed_ref, after_ref, first_ref, values_ref, grad_first_ref, grad_values_ref, total_ref
 ):
+    tokens = grad_mixed_ref.shape[1]
+    row_ids, lane_ids = lower_mask(tokens)
+    keep = jnp.where(lane_ids >= row_ids, 1.0, 0.0).astype(narrow)
     for number in range(base_ref.shape[0]):
         rows = slice(number * size, (number + 1) * size)
         extended = jnp.concatenate([grad_mixed_ref[rows], after_ref[rows]], axis=1)
-        band = rolled_rows(base_ref[number : number + 1, :], grad_mixed_ref.shape[1])
+        whole = rolled_rows(base_ref[number : number + 1, :], tokens)
+        near = whole * keep
+        band = jnp.concatenate([near, whole - near], axis=1)
         total_ref[rows] = lax.dot_general(
             extended, band, (((1,), (1,)), ((), ())), preferred_element_type=wide
         )
@@ -218,7 +240,7 @@
 
     by_token = pl.BlockSpec((tokens, width), lambda i: (0, i))
     by_channel = pl.BlockSpec((width, tokens), lambda i: (i, 0))
-    base_block = pl.BlockSpec((step_groups, 2 * tokens), lambda i: (i, 0))
+    base_block = pl.BlockSpec((step_groups, tokens), lambda i: (i, 0))
     channel_shape = (channels, tokens)
 
     gated = pl.pallas_call(
@@ -261,20 +283,11 @@
             compiler_params=params,
             cost_estimate=cost(5, channels),
         )(cotangent, output_gate, long_filter.T.reshape(ctx, own, tokens))
-    slab, prior = lax.optimization_barrier((slab, prior))
     slab_all = swapped(slab)
 
     turned = medium_filter.T.astype(wide)
-    pad = 2 * tokens - taps
-    forward_base = jnp.concatenate(
-        [
-            jnp.zeros((groups, tokens + 1 - taps), wide),
-            turned[:, ::-1],
-            jnp.zeros((groups, tokens - 1), wide),
-        ],
-        axis=1,
-    )
-    reverse_base = jnp.concatenate([turned, jnp.zeros((groups, pad), wide)], axis=1)
+    reverse_base = jnp.concatenate([turned, jnp.zeros((groups, tokens - taps), wide)], axis=1)
+    forward_base = jnp.concatenate([reverse_base[:, :1], reverse_base[:, :0:-1]], axis=1)
 
     mixed, carried = pl.pallas_call(
         functools.partial(forward_kernel, size),
@@ -285,8 +298,8 @@
         compiler_params=params,
         cost_estimate=cost(15, channels),
     )(forward_base, prior, gated, second_gate)
+    carried_all = swapped(carried.reshape(ctx, slab_width, tokens))
     carried, slab_all = lax.optimization_barrier((carried, slab_all))
-    carried_all = swapped(carried.reshape(ctx, slab_width, tokens))
 
     length = ctx * tokens
     filter_rows = slab_all[:, slab_width:].transpose(1, 0, 2).reshape(own, 1, length).astype(wide)
@@ -327,25 +340,35 @@
         cost_estimate=cost(23, channels),
     )(filter_rows, carried_all, slab_all)
     ahead_all, long_rows, back = lax.optimization_barrier((ahead_all, long_rows, back))
-    ahead = swapped(ahead_all).reshape(channel_shape)
-
-    grad_second, grad_mixed, sums = pl.pallas_call(
-        functools.partial(mixed_grad_kernel, size),
-        grid=steps,
-        in_specs=[by_channel, by_token, by_channel, by_channel, by_channel],
-        out_specs=[by_token, by_channel, base_block],
+    grad_second, grad_mixed, grad_token = pl.pallas_call(
+        mixed_grad_kernel,
+        grid=steps,
+        in_specs=[by_channel, by_token, by_channel],
+        out_specs=[by_token, by_channel, by_token],
         out_shape=[
             shape_of((tokens, channels), narrow),
             shape_of(channel_shape, narrow),
-            shape_of((groups, 2 * tokens), wide),
+            shape_of((tokens, channels), narrow),
         ],
         compiler_params=params,
-        cost_estimate=cost(20, channels),
-    )(back, second_gate, mixed, gated, prior)
-    ahead, grad_mixed, sums = lax.optimization_barrier((ahead, grad_mixed, sums))
+        cost_estimate=cost(7, channels),
+    )(back, second_gate, mixed)
     after = lax.ppermute(grad_mixed, "ctx", [(i + 1, i) for i in range(ctx - 1)])
-
-    terms = sums[:, tokens + 1 - taps : tokens + 1][:, ::-1] * scale
+    ahead_all, grad_token = lax.optimization_barrier((ahead_all, grad_token))
+    ahead = swapped(ahead_all).reshape(channel_shape)
+    sums = pl.pallas_call(
+        functools.partial(medium_kernel, size),
+        grid=steps,
+        in_specs=[by_token, by_channel, by_channel],
+        out_specs=base_block,
+        out_shape=shape_of((groups, tokens), wide),
+        compiler_params=params,
+        cost_estimate=cost(14, channels),
+    )(grad_token, gated, prior)
+
+    folded = jnp.concatenate([sums[:, :1], sums[:, :0:-1]], axis=1)
+    folded, ahead = lax.optimization_barrier((folded, ahead))
+    terms = folded[:, :taps] * scale
     long_pieces = long_rows.reshape(own, ctx, tokens).transpose(1, 0, 2).astype(wide)
     filter_terms = swapped(
         jnp.concatenate([terms.reshape(ctx, own, taps), long_pieces], axis=2)
@@ -354,17 +377,18 @@
     medium_own = jnp.sum(filter_terms[:, :, :taps], axis=0)
     squares = jnp.sum(jnp.square(medium_own)) + jnp.sum(jnp.square(long_rows.astype(wide)))
     package = jnp.concatenate([medium_own, jnp.full((1, taps), squares, wide)], axis=0)
-    grad_output_gate = pl.pallas_call(
-        output_grad_kernel,
-        grid=steps,
-        in_specs=[by_channel, by_token],
-        out_specs=by_token,
-        out_shape=shape_of((tokens, channels), narrow),
-        compiler_params=params,
-        cost_estimate=cost(6, channels),
-    )(ahead, cotangent)
-    package, after, grad_output_gate = lax.optimization_barrier(
-        (package, after, grad_output_gate)
+    grad_first, grad_values = pl.pallas_call(
+        functools.partial(gate_grad_kernel, size),
+        grid=steps,
+        in_specs=[base_block, by_channel, by_channel, by_token, by_token],
+        out_specs=[by_token] * 2,
+        out_shape=[shape_of((tokens, channels), narrow)] * 2,
+        scratch_shapes=[pltpu.VMEM((width, tokens), wide)],
+        compiler_params=params,
+        cost_estimate=cost(15, channels),
+    )(reverse_base, grad_mixed, after, first_gate, values)
+    package, grad_first, grad_values, ahead = lax.optimization_barrier(
+        (package, grad_first, grad_values, ahead)
     )
     ch = lax.axis_size("ch")
     gathered = lax.all_to_all(
@@ -379,16 +403,15 @@
     total = jnp.sum(gathered[:, :, own, 0])
     filter_rms = jnp.sqrt(total / ((length + taps) * groups * ch))
 
-    grad_first, grad_values = pl.pallas_call(
-        functools.partial(gate_grad_kernel, size),
-        grid=steps,
-        in_specs=[base_block, by_channel, by_channel, by_token, by_token],
-        out_specs=[by_token] * 2,
-        out_shape=[shape_of((tokens, channels), narrow)] * 2,
-        scratch_shapes=[pltpu.VMEM((width, tokens), wide)],
-        compiler_params=params,
-        cost_estimate=cost(15, channels),
-    )(reverse_base, grad_mixed, after, first_gate, values)
+    grad_output_gate = pl.pallas_call(
+        output_grad_kernel,
+        grid=steps,
+        in_specs=[by_channel, by_token],
+        out_specs=by_token,
+        out_shape=shape_of((tokens, channels), narrow),
+        compiler_params=params,
+        cost_estimate=cost(6, channels),
+    )(ahead, cotangent)
     return (
         grad_first,
         grad_second,

time: 226 us -> 232 us (1.027)
  starting transfers between devices: 47 us -> 63 us
  waiting for transfers between devices: 56.8 us -> 42.1 us
  other arithmetic: 4.06 us -> 8.38 us
  Pallas kernels: 97.7 us -> 93.5 us
  local copies, waits for them, and re-layouts: 14 us -> 17 us
    all_to_all x5, waiting for transfers between devices: 41 us -> 17.5 us  [swapped(): return lax.all_to_all(array, 'ctx', split_axis=0, concat_axis=0, tiled=True)]
    all_to_all x1, starting transfers between devices: 4.85 us -> 18.2 us  [body(): lax.all_to_all(jnp.broadcast_to(package[None], (ctx * ch, own + 1, taps))...]
    all_to_all x1, waiting for transfers between devices: 0.01 us -> 5.69 us  [body(): lax.all_to_all(jnp.broadcast_to(package[None], (ctx * ch, own + 1, taps))...]
    pallas_call x1, Pallas kernels: 5.89 us -> 1.63 us  [body(): pl.pallas_call(gated_kernel, grid=steps, in_specs=[by_token] * 2, out_spe...]
    ppermute x1, waiting for transfers between devices: 0.01 us -> 3.58 us  [body(): lax.ppermute(grad_mixed, 'ctx', [(i + 1, i) for i in range(ctx - 1)])]
    all_to_all x5, starting transfers between devices: 34.9 us -> 37.7 us  [swapped(): return lax.all_to_all(array, 'ctx', split_axis=0, concat_axis=0, tiled=True)]
    unnamed x35 -> x43, local copies, waits for them, and re-layouts: 9.58 us -> 12.3 us
    concatenate x1 -> x2, other arithmetic: 0.14 us -> 2.67 us  [the longest x1 1.66 us: body(): folded = jnp.concatenate([sums[:, :1], sums[:, :0:-1]], axis=1)]
  transfers between devices with their start and end apart: 8 -> 8, of which waited for: 5 -> 7; matrix products, arithmetic and copies ran while one was open for 3% -> 5% of each run, Pallas kernels for 41% -> 36%
where the time goes in v3:
time: 232 us; the launch traced here: 228 us
  Pallas kernels  93.5 us (40%)
  starting transfers between devices  63 us (27%)
  waiting for transfers between devices  42.1 us (18%)
  local copies, waits for them, and re-layouts  17 us (7%)
  other arithmetic  8.38 us (4%)
  between operations  4.06 us (2%)
    all_to_all x5, starting transfers between devices, swapped(): return lax.all_to_all(array, 'ctx', split_axis=0, concat_axis=0, tiled=True)  37.7 us
    pallas_call x1, Pallas kernels, body(): pl.pallas_call(functools.partial(ahead_kernel, scale), grid=(own,), in_sp...  20.1 us
    all_to_all x1, starting transfers between devices, body(): lax.all_to_all(jnp.broadcast_to(package[None], (ctx * ch, own + 1, taps))...  18.2 us
    all_to_all x5, waiting for transfers between devices, swapped(): return lax.all_to_all(array, 'ctx', split_axis=0, concat_axis=0, tiled=True)  17.5 us
    ppermute x1, waiting for transfers between devices, body(): prior = lax.ppermute(gated, 'ctx', [(i, i + 1) for i in range(ctx - 1)])  15.3 us
    pallas_call x1, Pallas kernels, body(): pl.pallas_call(functools.partial(gate_grad_kernel, size), grid=steps, in_...  14.5 us
    pallas_call x1, Pallas kernels, body(): pl.pallas_call(functools.partial(medium_kernel, size), grid=steps, in_spe...  13.8 us
    pallas_call x1, Pallas kernels, body(): pl.pallas_call(functools.partial(forward_kernel, size), grid=steps, in_sp...  13.1 us
  transfers between devices with their start and end apart: 8, of which 7 were waited for; matrix products, arithmetic and copies ran while one was open for 5% of the time, Pallas kernels for 36%

profile of v3, /device:TPU:0, one launch (start us, length us, event | category | flops | bytes accessed | tf_op | source)
XLA Modules:
  0.0 228.0 jit_solution(16337051635539164913)
XLA Ops:
  0.7 1.3 copy-done.6
  2.0 1.2 copy-done.8
  3.2 1.6 shard_map.126.gated_ref
  4.8 5.8 %collective-permute-start = (bf16[4096,128]{1,0:T(8,128)(2,1)S(1)}, bf16[4096,128]{1,0:T(8,128)(2,1)}, u32[]{:S(2)}, u32[]{:S(2)}) collective-permute-start(bf16[4096,128]{1,0:T(8,128)(2,1)S(1)} %shard_map.126.gated_ref), channel_id=1, source_target_pairs={{0,2},{2,4},{4,6},{6,8},{8,10},{10,12},{12,14},{14,16},{16,18},{18... | collective-permute-start | bytes 3145736 | tf_op jit(solution)/shard_map/ppermute | solution.py:255
  10.8 5.9 %shard_map.128 = bf16[16,272,128]{2,1,0:T(8,128)(2,1)} custom-call(bf16[128,4096]{1,0:T(8,128)(2,1)S(1)} %copy-done.10, bf16[128,4096]{1,0:T(8,128)(2,1)S(1)} %copy-done.3, bf16[16,16,128]{2,1,0:T(8,128)(2,1)S(1)} %bitcast.31), custom_call_target="tpu_custom_call" | custom-call | flops 5500000256 | tf_op jit(solution)/shard_map/pallas_call | solution.py:273
  16.7 5.1 %all-to-all-start = ((bf16[16,272,128]{2,1,0:T(8,128)(2,1)}), bf16[16,272,128]{2,1,0:T(8,128)(2,1)S(1)}, u32[]{:S(2)}, u32[]{:S(2)}) async-start(bf16[16,272,128]{2,1,0:T(8,128)(2,1)} %shard_map.128), calls=%async_computation | async-start | bytes 2228224 | tf_op jit(solution)/shard_map/all_to_all | solution.py:258
  22.9 1.0 pad_maximum_fusion.1.base_ref
  23.9 15.3 %collective-permute-done.prior_ref = bf16[4096,128]{1,0:T(8,128)(2,1)} collective-permute-done((bf16[4096,128]{1,0:T(8,128)(2,1)S(1)}, bf16[4096,128]{1,0:T(8,128)(2,1)}, u32[]{:S(2)}, u32[]{:S(2)}) %collective-permute-start) | collective-permute-done | bytes 1048608 | tf_op jit(solution)/shard_map/ppermute | solution.py:255
  39.2 13.1 %shard_map.127 = (f32[4096,128]{1,0:T(8,128)}, bf16[4096,128]{1,0:T(8,128)(2,1)}) custom-call(f32[256,128]{1,0:T(8,128)S(1)} %pad_maximum_fusion.1.base_ref, bf16[4096,128]{1,0:T(8,128)(2,1)} %collective-permute-done.prior_ref, bf16[4096,128]{1,0:T(8,128)(2,1)S(1)} %shard_map.126.gated_ref, bf16[128,4096]{1,0:T(8,128)(2,1)S(1)} %copy-done.4), custom_call_target="tpu_custom_call" | custom-call | flops 16499999744 | tf_op jit(solution)/shard_map/pallas_call | solution.py:292
  52.3 13.6 %all-to-all-start.1 = ((bf16[16,256,128]{2,1,0:T(8,128)(2,1)}), bf16[16,256,128]{2,1,0:T(8,128)(2,1)S(1)}, u32[]{:S(2)}, u32[]{:S(2)}) async-start(bf16[16,256,128]{2,1,0:T(8,128)(2,1)} %bitcast.5), calls=%async_computation.1 | async-start | bytes 2097152 | tf_op jit(solution)/shard_map/all_to_all | solution.py:258
  66.0 8.7 %shard_map.129 = bf16[16,256,128]{2,1,0:T(8,128)(2,1)S(1)} custom-call(f32[16,1,2048]{2,1,0:T(1,128)S(1)} %bitcast.29, bf16[16,272,128]{2,1,0:T(8,128)(2,1)S(1)} %all-to-all-done.inner_ref), custom_call_target="tpu_custom_call" | custom-call | flops 11000000512 | tf_op jit(solution)/shard_map/pallas_call | solution.py:314
  76.4 12.7 %all-to-all-done.1.carried_ref = bf16[16,256,128]{2,1,0:T(8,128)(2,1)S(1)} async-done(((bf16[16,256,128]{2,1,0:T(8,128)(2,1)}), bf16[16,256,128]{2,1,0:T(8,128)(2,1)S(1)}, u32[]{:S(2)}, u32[]{:S(2)}) %all-to-all-start.1) | async-done | bytes 1048608 | tf_op jit(solution)/shard_map/all_to_all | solution.py:258
  89.1 5.9 %all-to-all-start.2 = ((bf16[16,256,128]{2,1,0:T(8,128)(2,1)}), bf16[16,256,128]{2,1,0:T(8,128)(2,1)S(1)}, u32[]{:S(2)}, u32[]{:S(2)}) async-start(bf16[16,256,128]{2,1,0:T(8,128)(2,1)} %copy-done), calls=%async_computation.2 | async-start | bytes 2097152 | tf_op jit(solution)/shard_map/all_to_all | solution.py:258
  96.0 20.1 %shard_map.130 = (bf16[16,256,128]{2,1,0:T(8,128)(2,1)}, bf16[16,1,2048]{2,1,0:T(2,128)(2,1)S(1)}) custom-call(f32[16,1,2048]{2,1,0:T(1,128)S(1)} %bitcast.30, bf16[16,256,128]{2,1,0:T(8,128)(2,1)S(1)} %all-to-all-done.1.carried_ref, bf16[16,272,128]{2,1,0:T(8,128)(2,1)S(1)} %all-to-all-done.inner_ref), custom_call_target="tpu_custom_call" | custom-call | flops 25300000768 | tf_op jit(solution)/shard_map/pallas_call | solution.py:328
  116.1 1.8 all-to-all-done.2
  117.9 1.2 copy-done.5
  119.1 10.0 %shard_map.131 = (bf16[128,4096]{1,0:T(8,128)(2,1)}, bf16[4096,128]{1,0:T(8,128)(2,1)S(1)}, bf16[128,4096]{1,0:T(8,128)(2,1)S(1)}) custom-call(bf16[4096,128]{1,0:T(8,128)(2,1)S(1)} %bitcast.27, bf16[128,4096]{1,0:T(8,128)(2,1)S(1)} %copy-done.5, f32[4096,128]{1,0:T(8,128)} %get-tuple-element.38.mixed_ref), custom_call_target="tpu_custom_call" | custom-call | flops 7699999744 | tf_op jit(solution)/shard_map/pallas_call | solution.py:343
  129.1 1.0 copy-done.14
  131.0 6.1 %all-to-all-start.3 = ((bf16[16,256,128]{2,1,0:T(8,128)(2,1)}), bf16[16,256,128]{2,1,0:T(8,128)(2,1)S(1)}, u32[]{:S(2)}, u32[]{:S(2)}) async-start(bf16[16,256,128]{2,1,0:T(8,128)(2,1)} %get-tuple-element.41), calls=%async_computation.3 | async-start | bytes 2097152 | tf_op jit(solution)/shard_map/all_to_all | solution.py:258
  137.2 1.3 collective-permute-start.1
  138.5 1.2 copy-done.17
  139.7 13.8 %shard_map.132 = f32[256,128]{1,0:T(8,128)S(1)} custom-call(bf16[128,4096]{1,0:T(8,128)(2,1)S(1)} %copy-done.17, bf16[4096,128]{1,0:T(8,128)(2,1)S(1)} %copy-done.13, bf16[4096,128]{1,0:T(8,128)(2,1)} %collective-permute-done.prior_ref), custom_call_target="tpu_custom_call" | custom-call | flops 15399999488 | tf_op jit(solution)/shard_map/pallas_call | solution.py:359
  155.3 1.7 pad_maximum_fusion.2
  157.8 2.2 all-to-all-done.3
  161.0 1.6 pad_maximum_fusion
  162.6 6.9 %all-to-all-start.4 = ((f32[16,16,256]{2,1,0:T(8,128)}), f32[16,16,256]{2,1,0:T(8,128)}, u32[]{:S(2)}, u32[]{:S(2)}) async-start(f32[16,16,256]{2,1,0:T(8,128)} %pad_maximum_fusion), calls=%async_computation.4 | async-start | bytes 524288 | tf_op jit(solution)/shard_map/all_to_all | solution.py:258
  169.5 3.6 %collective-permute-done.1.after_ref = bf16[4096,128]{1,0:T(8,128)(2,1)} collective-permute-done((bf16[4096,128]{1,0:T(8,128)(2,1)S(1)}, bf16[4096,128]{1,0:T(8,128)(2,1)}, u32[]{:S(2)}, u32[]{:S(2)}) %collective-permute-start.1) | collective-permute-done | bytes 1048608 | tf_op jit(solution)/shard_map/ppermute | solution.py:356
  173.1 1.2 copy-done.9
  174.3 14.5 %shard_map.133 = (bf16[128,4096]{1,0:T(8,128)(2,1)}, bf16[128,4096]{1,0:T(8,128)(2,1)}) custom-call(f32[256,128]{1,0:T(8,128)S(1)} %convert_bitcast_fusion.1.base_ref, bf16[4096,128]{1,0:T(8,128)(2,1)S(1)} %copy-done.15, bf16[4096,128]{1,0:T(8,128)(2,1)} %collective-permute-done.1.after_ref, bf16[128,4096]{1,0:T(8,128)(2,1)S(1)} %copy-done.7, ...), custom_call_target="tpu_custom_call" | custom-call | flops 16499999744 | tf_op jit(solution)/shard_map/pallas_call | solution.py:380
  193.2 18.2 %all-to-all-start.5 = ((f32[32,17,128]{2,1,0:T(8,128)}), f32[32,17,128]{2,1,0:T(8,128)S(1)}, u32[]{:S(2)}, u32[]{:S(2)}) async-start(f32[32,17,128]{2,1,0:T(8,128)} %broadcast_in_dim.2), calls=%async_computation.5 | async-start | bytes 786432 | tf_op jit(solution)/shard_map/all_to_all | solution.py:394
  213.1 5.8 %shard_map.134 = bf16[128,4096]{1,0:T(8,128)(2,1)} custom-call(bf16[4096,128]{1,0:T(8,128)(2,1)S(1)} %bitcast.26, bf16[128,4096]{1,0:T(8,128)(2,1)S(1)} %copy-done.11), custom_call_target="tpu_custom_call" | custom-call | flops 6600000000 | tf_op jit(solution)/shard_map/pallas_call | solution.py:406
  218.9 5.7 %all-to-all-done.5 = f32[32,17,128]{2,1,0:T(8,128)S(1)} async-done(((f32[32,17,128]{2,1,0:T(8,128)}), f32[32,17,128]{2,1,0:T(8,128)S(1)}, u32[]{:S(2)}, u32[]{:S(2)}) %all-to-all-start.5) | async-done | bytes 278560 | tf_op jit(solution)/shard_map/all_to_all | solution.py:394
  (61 shorter events, 14.6 us)
Async XLA Ops:
  0.6 10.1 %copy-start.3 = (bf16[128,4096]{1,0:T(8,128)(2,1)S(1)}, bf16[128,4096]{1,0:T(8,128)(2,1)}, u32[]{:S(2)}) copy-start(bf16[128,4096]{1,0:T(8,128)(2,1)} %output_ref.1) | copy-start | bytes 3145732
  0.6 1.3 copy-start.6
  2.0 1.2 copy-start.8
  3.2 7.5 %copy-start.18 = (bf16[128,256]{1,0:T(8,128)(2,1)S(1)}, bf16[128,256]{1,0:T(8,128)(2,1)}, u32[]{:S(2)}) copy-start(bf16[128,256]{1,0:T(8,128)(2,1)} %param.13) | copy-start | bytes 196612
  3.2 7.6 %copy-start.10 = (bf16[128,4096]{1,0:T(8,128)(2,1)S(1)}, bf16[128,4096]{1,0:T(8,128)(2,1)}, u32[]{:S(2)}) copy-start(bf16[128,4096]{1,0:T(8,128)(2,1)} %cotangent_ref.3) | copy-start | bytes 3145732
  4.8 34.4 %copy-start.12 = (bf16[4096,128]{1,0:T(8,128)(2,1)}, bf16[4096,128]{1,0:T(8,128)(2,1)S(1)}, u32[]{:S(2)}) copy-start(bf16[4096,128]{1,0:T(8,128)(2,1)S(1)} %shard_map.126.gated_ref) | copy-start | bytes 3145732
  4.8 34.4 %collective-permute-start = (bf16[4096,128]{1,0:T(8,128)(2,1)S(1)}, bf16[4096,128]{1,0:T(8,128)(2,1)}, u32[]{:S(2)}, u32[]{:S(2)}) collective-permute-start(bf16[4096,128]{1,0:T(8,128)(2,1)S(1)} %shard_map.126.gated_ref), channel_id=1, source_target_pairs={{0,2},{2,4},{4,6},{6,8},{8,10},{10,12},{12,14},{14,16},{16,18},{18... | collective-permute-start | bytes 3145736 | tf_op jit(solution)/shard_map/ppermute | solution.py:255
  16.7 5.1 %copy-start.19 = (bf16[128,256]{1,0:T(8,128)(2,1)S(1)}, bf16[128,256]{1,0:T(8,128)(2,1)}, u32[]{:S(2)}) copy-start(bf16[128,256]{1,0:T(8,128)(2,1)} %param.12) | copy-start | bytes 196612
  16.7 35.6 %all-to-all-start = ((bf16[16,272,128]{2,1,0:T(8,128)(2,1)}), bf16[16,272,128]{2,1,0:T(8,128)(2,1)S(1)}, u32[]{:S(2)}, u32[]{:S(2)}) async-start(bf16[16,272,128]{2,1,0:T(8,128)(2,1)} %shard_map.128), calls=%async_computation | async-start | bytes 2228224 | tf_op jit(solution)/shard_map/all_to_all | solution.py:258
  21.8 17.4 %copy-start.4 = (bf16[128,4096]{1,0:T(8,128)(2,1)S(1)}, bf16[128,4096]{1,0:T(8,128)(2,1)}, u32[]{:S(2)}) copy-start(bf16[128,4096]{1,0:T(8,128)(2,1)} %second_ref.3) | copy-start | bytes 3145732
  52.3 36.8 %all-to-all-start.1 = ((bf16[16,256,128]{2,1,0:T(8,128)(2,1)}), bf16[16,256,128]{2,1,0:T(8,128)(2,1)S(1)}, u32[]{:S(2)}, u32[]{:S(2)}) async-start(bf16[16,256,128]{2,1,0:T(8,128)(2,1)} %bitcast.5), calls=%async_computation.1 | async-start | bytes 2097152 | tf_op jit(solution)/shard_map/all_to_all | solution.py:258
  74.7 1.0 copy-start
  75.7 0.7 copy-start.1
  89.1 28.8 %all-to-all-start.2 = ((bf16[16,256,128]{2,1,0:T(8,128)(2,1)}), bf16[16,256,128]{2,1,0:T(8,128)(2,1)S(1)}, u32[]{:S(2)}, u32[]{:S(2)}) async-start(bf16[16,256,128]{2,1,0:T(8,128)(2,1)} %copy-done), calls=%async_computation.2 | async-start | bytes 2097152 | tf_op jit(solution)/shard_map/all_to_all | solution.py:258
  95.0 0.9 copy-start.2
  117.9 1.2 copy-start.5
  129.1 1.0 copy-start.14
  130.0 1.0 copy-start.16
  131.0 7.5 %copy-start.13 = (bf16[4096,128]{1,0:T(8,128)(2,1)S(1)}, bf16[4096,128]{1,0:T(8,128)(2,1)}, u32[]{:S(2)}) copy-start(bf16[4096,128]{1,0:T(8,128)(2,1)} %copy-done.12) | copy-start | bytes 3145732
  131.0 6.2 %copy-start.15 = (bf16[4096,128]{1,0:T(8,128)(2,1)S(1)}, bf16[4096,128]{1,0:T(8,128)(2,1)}, u32[]{:S(2)}) copy-start(bf16[4096,128]{1,0:T(8,128)(2,1)} %copy-done.14) | copy-start | bytes 3145732
  131.0 29.0 %all-to-all-start.3 = ((bf16[16,256,128]{2,1,0:T(8,128)(2,1)}), bf16[16,256,128]{2,1,0:T(8,128)(2,1)S(1)}, u32[]{:S(2)}, u32[]{:S(2)}) async-start(bf16[16,256,128]{2,1,0:T(8,128)(2,1)} %get-tuple-element.41), calls=%async_computation.3 | async-start | bytes 2097152 | tf_op jit(solution)/shard_map/all_to_all | solution.py:258
  137.2 35.9 %collective-permute-start.1 = (bf16[4096,128]{1,0:T(8,128)(2,1)S(1)}, bf16[4096,128]{1,0:T(8,128)(2,1)}, u32[]{:S(2)}, u32[]{:S(2)}) collective-permute-start(bf16[4096,128]{1,0:T(8,128)(2,1)S(1)} %copy-done.15), channel_id=1, source_target_pairs={{2,0},{4,2},{6,4},{8,6},{10,8},{12,10},{14,12},{16,14},{18,16},{20... | collective-permute-start | bytes 3145736 | tf_op jit(solution)/shard_map/ppermute | solution.py:356
  138.5 1.2 copy-start.17
  154.6 18.5 %copy-start.7 = (bf16[128,4096]{1,0:T(8,128)(2,1)S(1)}, bf16[128,4096]{1,0:T(8,128)(2,1)}, u32[]{:S(2)}) copy-start(bf16[128,4096]{1,0:T(8,128)(2,1)} %first_ref.3) | copy-start | bytes 3145732
  162.6 27.0 %all-to-all-start.4 = ((f32[16,16,256]{2,1,0:T(8,128)}), f32[16,16,256]{2,1,0:T(8,128)}, u32[]{:S(2)}, u32[]{:S(2)}) async-start(f32[16,16,256]{2,1,0:T(8,128)} %pad_maximum_fusion), calls=%async_computation.4 | async-start | bytes 524288 | tf_op jit(solution)/shard_map/all_to_all | solution.py:258
  173.1 1.2 copy-start.9
  188.8 24.2 %copy-start.11 = (bf16[128,4096]{1,0:T(8,128)(2,1)S(1)}, bf16[128,4096]{1,0:T(8,128)(2,1)}, u32[]{:S(2)}) copy-start(bf16[128,4096]{1,0:T(8,128)(2,1)} %cotangent_ref.3) | copy-start | bytes 3145732
  193.2 31.4 %all-to-all-start.5 = ((f32[32,17,128]{2,1,0:T(8,128)}), f32[32,17,128]{2,1,0:T(8,128)S(1)}, u32[]{:S(2)}, u32[]{:S(2)}) async-start(f32[32,17,128]{2,1,0:T(8,128)} %broadcast_in_dim.2), calls=%async_computation.5 | async-start | bytes 786432 | tf_op jit(solution)/shard_map/all_to_all | solution.py:394

commit v4 on v3

--- a/solution.py
+++ b/solution.py
@@ -377,18 +377,17 @@
     medium_own = jnp.sum(filter_terms[:, :, :taps], axis=0)
     squares = jnp.sum(jnp.square(medium_own)) + jnp.sum(jnp.square(long_rows.astype(wide)))
     package = jnp.concatenate([medium_own, jnp.full((1, taps), squares, wide)], axis=0)
-    grad_first, grad_values = pl.pallas_call(
-        functools.partial(gate_grad_kernel, size),
-        grid=steps,
-        in_specs=[base_block, by_channel, by_channel, by_token, by_token],
-        out_specs=[by_token] * 2,
-        out_shape=[shape_of((tokens, channels), narrow)] * 2,
-        scratch_shapes=[pltpu.VMEM((width, tokens), wide)],
-        compiler_params=params,
-        cost_estimate=cost(15, channels),
-    )(reverse_base, grad_mixed, after, first_gate, values)
-    package, grad_first, grad_values, ahead = lax.optimization_barrier(
-        (package, grad_first, grad_values, ahead)
+    grad_output_gate = pl.pallas_call(
+        output_grad_kernel,
+        grid=steps,
+        in_specs=[by_channel, by_token],
+        out_specs=by_token,
+        out_shape=shape_of((tokens, channels), narrow),
+        compiler_params=params,
+        cost_estimate=cost(6, channels),
+    )(ahead, cotangent)
+    package, after, grad_output_gate = lax.optimization_barrier(
+        (package, after, grad_output_gate)
     )
     ch = lax.axis_size("ch")
     gathered = lax.all_to_all(
@@ -403,15 +402,16 @@
     total = jnp.sum(gathered[:, :, own, 0])
     filter_rms = jnp.sqrt(total / ((length + taps) * groups * ch))
 
-    grad_output_gate = pl.pallas_call(
-        output_grad_kernel,
-        grid=steps,
-        in_specs=[by_channel, by_token],
-        out_specs=by_token,
-        out_shape=shape_of((tokens, channels), narrow),
-        compiler_params=params,
-        cost_estimate=cost(6, channels),
-    )(ahead, cotangent)
+    grad_first, grad_values = pl.pallas_call(
+        functools.partial(gate_grad_kernel, size),
+        grid=steps,
+        in_specs=[base_block, by_channel, by_channel, by_token, by_token],
+        out_specs=[by_token] * 2,
+        out_shape=[shape_of((tokens, channels), narrow)] * 2,
+        scratch_shapes=[pltpu.VMEM((width, tokens), wide)],
+        compiler_params=params,
+        cost_estimate=cost(15, channels),
+    )(reverse_base, grad_mixed, after, first_gate, values)
     return (
         grad_first,
         grad_second,

time: 232 us -> 221 us (0.953)
  starting transfers between devices: 63 us -> 48.7 us
  waiting for transfers between devices: 42.1 us -> 52.5 us
  local copies, waits for them, and re-layouts: 17 us -> 13.3 us
  other arithmetic: 8.38 us -> 5.02 us
    all_to_all x5, waiting for transfers between devices: 17.5 us -> 37.2 us  [swapped(): return lax.all_to_all(array, 'ctx', split_axis=0, concat_axis=0, tiled=True)]
    all_to_all x1, starting transfers between devices: 18.2 us -> 4.23 us  [body(): lax.all_to_all(jnp.broadcast_to(package[None], (ctx * ch, own + 1, taps))...]
    all_to_all x1, waiting for transfers between devices: 5.69 us -> 0.01 us  [body(): lax.all_to_all(jnp.broadcast_to(package[None], (ctx * ch, own + 1, taps))...]
    ppermute x1, waiting for transfers between devices: 3.58 us -> 0.01 us  [body(): lax.ppermute(grad_mixed, 'ctx', [(i + 1, i) for i in range(ctx - 1)])]
    unnamed x43 -> x39, local copies, waits for them, and re-layouts: 12.3 us -> 8.97 us
  transfers between devices with their start and end apart: 8 -> 8, of which waited for: 7 -> 5; matrix products, arithmetic and copies ran while one was open for 5% -> 3% of each run, Pallas kernels for 36% -> 38%
where the time goes in v4:
time: 221 us; the launch traced here: 218 us
  Pallas kernels  94.1 us (43%)
  waiting for transfers between devices  52.5 us (24%)
  starting transfers between devices  48.7 us (22%)
  local copies, waits for them, and re-layouts  13.3 us (6%)
  other arithmetic  5.02 us (2%)
  between operations  4.11 us (2%)
    all_to_all x5, starting transfers between devices, swapped(): return lax.all_to_all(array, 'ctx', split_axis=0, concat_axis=0, tiled=True)  37.3 us
    all_to_all x5, waiting for transfers between devices, swapped(): return lax.all_to_all(array, 'ctx', split_axis=0, concat_axis=0, tiled=True)  37.2 us
    pallas_call x1, Pallas kernels, body(): pl.pallas_call(functools.partial(ahead_kernel, scale), grid=(own,), in_sp...  20.1 us
    ppermute x1, waiting for transfers between devices, body(): prior = lax.ppermute(gated, 'ctx', [(i, i + 1) for i in range(ctx - 1)])  15.3 us
    pallas_call x1, Pallas kernels, body(): pl.pallas_call(functools.partial(gate_grad_kernel, size), grid=steps, in_...  14.8 us
    pallas_call x1, Pallas kernels, body(): pl.pallas_call(functools.partial(medium_kernel, size), grid=steps, in_spe...  13.8 us
    pallas_call x1, Pallas kernels, body(): pl.pallas_call(functools.partial(forward_kernel, size), grid=steps, in_sp...  13.1 us
    pallas_call x1, Pallas kernels, body(): pl.pallas_call(mixed_grad_kernel, grid=steps, in_specs=[by_channel, by_to...  10.2 us
  transfers between devices with their start and end apart: 8, of which 5 were waited for; matrix products, arithmetic and copies ran while one was open for 3% of the time, Pallas kernels for 38%

profile of v4, /device:TPU:0, one launch (start us, length us, event | category | flops | bytes accessed | tf_op | source)
XLA Modules:
  0.0 217.8 jit_solution(13640410482348035020)
XLA Ops:
  0.7 1.4 copy-done.8
  2.0 1.2 copy-done.10
  3.3 1.6 shard_map.126.gated_ref
  4.9 5.8 %collective-permute-start = (bf16[4096,128]{1,0:T(8,128)(2,1)S(1)}, bf16[4096,128]{1,0:T(8,128)(2,1)}, u32[]{:S(2)}, u32[]{:S(2)}) collective-permute-start(bf16[4096,128]{1,0:T(8,128)(2,1)S(1)} %shard_map.126.gated_ref), channel_id=1, source_target_pairs={{0,2},{2,4},{4,6},{6,8},{8,10},{10,12},{12,14},{14,16},{16,18},{18... | collective-permute-start | bytes 3145736 | tf_op jit(solution)/shard_map/ppermute | solution.py:255
  10.9 5.9 %shard_map.128 = bf16[16,272,128]{2,1,0:T(8,128)(2,1)} custom-call(bf16[128,4096]{1,0:T(8,128)(2,1)S(1)} %copy-done.6, bf16[128,4096]{1,0:T(8,128)(2,1)S(1)} %copy-done.3, bf16[16,16,128]{2,1,0:T(8,128)(2,1)S(1)} %bitcast.31), custom_call_target="tpu_custom_call" | custom-call | flops 5500000256 | tf_op jit(solution)/shard_map/pallas_call | solution.py:273
  16.7 5.1 %all-to-all-start = ((bf16[16,272,128]{2,1,0:T(8,128)(2,1)}), bf16[16,272,128]{2,1,0:T(8,128)(2,1)S(1)}, u32[]{:S(2)}, u32[]{:S(2)}) async-start(bf16[16,272,128]{2,1,0:T(8,128)(2,1)} %shard_map.128), calls=%async_computation | async-start | bytes 2228224 | tf_op jit(solution)/shard_map/all_to_all | solution.py:258
  22.9 1.0 pad_maximum_fusion.1.base_ref
  23.9 15.3 %collective-permute-done.prior_ref = bf16[4096,128]{1,0:T(8,128)(2,1)} collective-permute-done((bf16[4096,128]{1,0:T(8,128)(2,1)S(1)}, bf16[4096,128]{1,0:T(8,128)(2,1)}, u32[]{:S(2)}, u32[]{:S(2)}) %collective-permute-start) | collective-permute-done | bytes 1048608 | tf_op jit(solution)/shard_map/ppermute | solution.py:255
  39.3 13.1 %shard_map.127 = (f32[4096,128]{1,0:T(8,128)}, bf16[4096,128]{1,0:T(8,128)(2,1)}) custom-call(f32[256,128]{1,0:T(8,128)S(1)} %pad_maximum_fusion.1.base_ref, bf16[4096,128]{1,0:T(8,128)(2,1)} %collective-permute-done.prior_ref, bf16[4096,128]{1,0:T(8,128)(2,1)S(1)} %shard_map.126.gated_ref, bf16[128,4096]{1,0:T(8,128)(2,1)S(1)} %copy-done.4), custom_call_target="tpu_custom_call" | custom-call | flops 16499999744 | tf_op jit(solution)/shard_map/pallas_call | solution.py:292
  52.4 13.6 %all-to-all-start.1 = ((bf16[16,256,128]{2,1,0:T(8,128)(2,1)}), bf16[16,256,128]{2,1,0:T(8,128)(2,1)S(1)}, u32[]{:S(2)}, u32[]{:S(2)}) async-start(bf16[16,256,128]{2,1,0:T(8,128)(2,1)} %bitcast.5), calls=%async_computation.1 | async-start | bytes 2097152 | tf_op jit(solution)/shard_map/all_to_all | solution.py:258
  66.1 8.7 %shard_map.129 = bf16[16,256,128]{2,1,0:T(8,128)(2,1)S(1)} custom-call(f32[16,1,2048]{2,1,0:T(1,128)S(1)} %bitcast.29, bf16[16,272,128]{2,1,0:T(8,128)(2,1)S(1)} %all-to-all-done.inner_ref), custom_call_target="tpu_custom_call" | custom-call | flops 11000000512 | tf_op jit(solution)/shard_map/pallas_call | solution.py:314
  74.8 1.0 copy-done
  76.4 12.7 %all-to-all-done.1.carried_ref = bf16[16,256,128]{2,1,0:T(8,128)(2,1)S(1)} async-done(((bf16[16,256,128]{2,1,0:T(8,128)(2,1)}), bf16[16,256,128]{2,1,0:T(8,128)(2,1)S(1)}, u32[]{:S(2)}, u32[]{:S(2)}) %all-to-all-start.1) | async-done | bytes 1048608 | tf_op jit(solution)/shard_map/all_to_all | solution.py:258
  89.2 5.9 %all-to-all-start.2 = ((bf16[16,256,128]{2,1,0:T(8,128)(2,1)}), bf16[16,256,128]{2,1,0:T(8,128)(2,1)S(1)}, u32[]{:S(2)}, u32[]{:S(2)}) async-start(bf16[16,256,128]{2,1,0:T(8,128)(2,1)} %copy-done), calls=%async_computation.2 | async-start | bytes 2097152 | tf_op jit(solution)/shard_map/all_to_all | solution.py:258
  95.1 0.9 copy-done.2
  96.0 20.1 %shard_map.130 = (bf16[16,256,128]{2,1,0:T(8,128)(2,1)}, bf16[16,1,2048]{2,1,0:T(2,128)(2,1)S(1)}) custom-call(f32[16,1,2048]{2,1,0:T(1,128)S(1)} %bitcast.30, bf16[16,256,128]{2,1,0:T(8,128)(2,1)S(1)} %all-to-all-done.1.carried_ref, bf16[16,272,128]{2,1,0:T(8,128)(2,1)S(1)} %all-to-all-done.inner_ref), custom_call_target="tpu_custom_call" | custom-call | flops 25300000768 | tf_op jit(solution)/shard_map/pallas_call | solution.py:328
  116.1 1.8 all-to-all-done.2
  118.0 1.2 copy-done.5
  119.2 10.2 %shard_map.131 = (bf16[128,4096]{1,0:T(8,128)(2,1)}, bf16[4096,128]{1,0:T(8,128)(2,1)}, bf16[128,4096]{1,0:T(8,128)(2,1)S(1)}) custom-call(bf16[4096,128]{1,0:T(8,128)(2,1)S(1)} %bitcast.27, bf16[128,4096]{1,0:T(8,128)(2,1)S(1)} %copy-done.5, f32[4096,128]{1,0:T(8,128)} %get-tuple-element.36.mixed_ref), custom_call_target="tpu_custom_call" | custom-call | flops 7699999744 | tf_op jit(solution)/shard_map/pallas_call | solution.py:343
  129.4 1.0 copy-done.14
  130.3 6.1 %all-to-all-start.3 = ((bf16[16,256,128]{2,1,0:T(8,128)(2,1)}), bf16[16,256,128]{2,1,0:T(8,128)(2,1)S(1)}, u32[]{:S(2)}, u32[]{:S(2)}) async-start(bf16[16,256,128]{2,1,0:T(8,128)(2,1)} %get-tuple-element.41), calls=%async_computation.3 | async-start | bytes 2097152 | tf_op jit(solution)/shard_map/all_to_all | solution.py:258
  136.5 13.8 %shard_map.132 = f32[256,128]{1,0:T(8,128)S(1)} custom-call(bf16[128,4096]{1,0:T(8,128)(2,1)S(1)} %copy-done.15, bf16[4096,128]{1,0:T(8,128)(2,1)S(1)} %copy-done.13, bf16[4096,128]{1,0:T(8,128)(2,1)} %collective-permute-done.prior_ref), custom_call_target="tpu_custom_call" | custom-call | flops 15399999488 | tf_op jit(solution)/shard_map/pallas_call | solution.py:359
  150.8 1.4 collective-permute-start.1
  153.2 6.1 %all-to-all-done.3 = bf16[16,256,128]{2,1,0:T(8,128)(2,1)S(1)} async-done(((bf16[16,256,128]{2,1,0:T(8,128)(2,1)}), bf16[16,256,128]{2,1,0:T(8,128)(2,1)S(1)}, u32[]{:S(2)}, u32[]{:S(2)}) %all-to-all-start.3) | async-done | bytes 1048608 | tf_op jit(solution)/shard_map/all_to_all | solution.py:258
  160.1 6.4 %all-to-all-start.4 = ((f32[16,16,256]{2,1,0:T(8,128)}), f32[16,16,256]{2,1,0:T(8,128)}, u32[]{:S(2)}, u32[]{:S(2)}) async-start(f32[16,16,256]{2,1,0:T(8,128)} %pad_maximum_fusion), calls=%async_computation.4 | async-start | bytes 524288 | tf_op jit(solution)/shard_map/all_to_all | solution.py:258
  166.6 5.8 %shard_map.133 = bf16[128,4096]{1,0:T(8,128)(2,1)} custom-call(bf16[4096,128]{1,0:T(8,128)(2,1)S(1)} %bitcast.26, bf16[128,4096]{1,0:T(8,128)(2,1)S(1)} %copy-done.7), custom_call_target="tpu_custom_call" | custom-call | flops 6600000000 | tf_op jit(solution)/shard_map/pallas_call | solution.py:380
  172.4 16.5 %all-to-all-done.4 = f32[16,16,256]{2,1,0:T(8,128)} async-done(((f32[16,16,256]{2,1,0:T(8,128)}), f32[16,16,256]{2,1,0:T(8,128)}, u32[]{:S(2)}, u32[]{:S(2)}) %all-to-all-start.4) | async-done | bytes 262176 | tf_op jit(solution)/shard_map/all_to_all | solution.py:258
  188.9 0.9 slice_reduce_fusion
  192.5 4.2 %all-to-all-start.5 = ((f32[32,17,128]{2,1,0:T(8,128)}), f32[32,17,128]{2,1,0:T(8,128)}, u32[]{:S(2)}, u32[]{:S(2)}) async-start(f32[32,17,128]{2,1,0:T(8,128)} %broadcast_in_dim.2), calls=%async_computation.5 | async-start | bytes 786432 | tf_op jit(solution)/shard_map/all_to_all | solution.py:393
  196.8 14.8 %shard_map.134 = (bf16[128,4096]{1,0:T(8,128)(2,1)}, bf16[128,4096]{1,0:T(8,128)(2,1)}) custom-call(f32[256,128]{1,0:T(8,128)S(1)} %convert_bitcast_fusion.1.base_ref, bf16[4096,128]{1,0:T(8,128)(2,1)} %get-tuple-element.37.grad_mixed_ref, bf16[4096,128]{1,0:T(8,128)(2,1)} %collective-permute-done.1.after_ref, bf16[128,4096]{1,0:T(8,128)(2,1)S(1)} %copy-done.9, ...), custom_call_target="tpu_custom_call" | custom-call | flops 16499999744 | tf_op jit(solution)/shard_map/pallas_call | solution.py:405
  211.6 0.9 slice.49
  213.3 1.1 copy.41
  (57 shorter events, 7.8 us)
Async XLA Ops:
  0.6 10.2 %copy-start.6 = (bf16[128,4096]{1,0:T(8,128)(2,1)S(1)}, bf16[128,4096]{1,0:T(8,128)(2,1)}, u32[]{:S(2)}) copy-start(bf16[128,4096]{1,0:T(8,128)(2,1)} %cotangent_ref.3) | copy-start | bytes 3145732
  0.6 10.2 %copy-start.3 = (bf16[128,4096]{1,0:T(8,128)(2,1)S(1)}, bf16[128,4096]{1,0:T(8,128)(2,1)}, u32[]{:S(2)}) copy-start(bf16[128,4096]{1,0:T(8,128)(2,1)} %output_ref.1) | copy-start | bytes 3145732
  0.7 1.4 copy-start.8
  2.0 1.2 copy-start.10
  3.3 7.5 %copy-start.16 = (bf16[128,256]{1,0:T(8,128)(2,1)S(1)}, bf16[128,256]{1,0:T(8,128)(2,1)}, u32[]{:S(2)}) copy-start(bf16[128,256]{1,0:T(8,128)(2,1)} %param.13) | copy-start | bytes 196612
  4.9 34.4 %copy-start.12 = (bf16[4096,128]{1,0:T(8,128)(2,1)}, bf16[4096,128]{1,0:T(8,128)(2,1)S(1)}, u32[]{:S(2)}) copy-start(bf16[4096,128]{1,0:T(8,128)(2,1)S(1)} %shard_map.126.gated_ref) | copy-start | bytes 3145732
  4.9 34.4 %collective-permute-start = (bf16[4096,128]{1,0:T(8,128)(2,1)S(1)}, bf16[4096,128]{1,0:T(8,128)(2,1)}, u32[]{:S(2)}, u32[]{:S(2)}) collective-permute-start(bf16[4096,128]{1,0:T(8,128)(2,1)S(1)} %shard_map.126.gated_ref), channel_id=1, source_target_pairs={{0,2},{2,4},{4,6},{6,8},{8,10},{10,12},{12,14},{14,16},{16,18},{18... | collective-permute-start | bytes 3145736 | tf_op jit(solution)/shard_map/ppermute | solution.py:255
  16.7 5.1 %copy-start.17 = (bf16[128,256]{1,0:T(8,128)(2,1)S(1)}, bf16[128,256]{1,0:T(8,128)(2,1)}, u32[]{:S(2)}) copy-start(bf16[128,256]{1,0:T(8,128)(2,1)} %param.12) | copy-start | bytes 196612
  16.7 35.7 %all-to-all-start = ((bf16[16,272,128]{2,1,0:T(8,128)(2,1)}), bf16[16,272,128]{2,1,0:T(8,128)(2,1)S(1)}, u32[]{:S(2)}, u32[]{:S(2)}) async-start(bf16[16,272,128]{2,1,0:T(8,128)(2,1)} %shard_map.128), calls=%async_computation | async-start | bytes 2228224 | tf_op jit(solution)/shard_map/all_to_all | solution.py:258
  21.9 17.4 %copy-start.4 = (bf16[128,4096]{1,0:T(8,128)(2,1)S(1)}, bf16[128,4096]{1,0:T(8,128)(2,1)}, u32[]{:S(2)}) copy-start(bf16[128,4096]{1,0:T(8,128)(2,1)} %second_ref.3) | copy-start | bytes 3145732
  52.4 36.8 %all-to-all-start.1 = ((bf16[16,256,128]{2,1,0:T(8,128)(2,1)}), bf16[16,256,128]{2,1,0:T(8,128)(2,1)S(1)}, u32[]{:S(2)}, u32[]{:S(2)}) async-start(bf16[16,256,128]{2,1,0:T(8,128)(2,1)} %bitcast.5), calls=%async_computation.1 | async-start | bytes 2097152 | tf_op jit(solution)/shard_map/all_to_all | solution.py:258
  74.8 1.0 copy-start
  75.8 0.7 copy-start.1
  89.2 28.8 %all-to-all-start.2 = ((bf16[16,256,128]{2,1,0:T(8,128)(2,1)}), bf16[16,256,128]{2,1,0:T(8,128)(2,1)S(1)}, u32[]{:S(2)}, u32[]{:S(2)}) async-start(bf16[16,256,128]{2,1,0:T(8,128)(2,1)} %copy-done), calls=%async_computation.2 | async-start | bytes 2097152 | tf_op jit(solution)/shard_map/all_to_all | solution.py:258
  95.1 0.9 copy-start.2
  118.0 1.2 copy-start.5
  129.4 1.0 copy-start.14
  130.3 6.2 %copy-start.13 = (bf16[4096,128]{1,0:T(8,128)(2,1)S(1)}, bf16[4096,128]{1,0:T(8,128)(2,1)}, u32[]{:S(2)}) copy-start(bf16[4096,128]{1,0:T(8,128)(2,1)} %copy-done.12) | copy-start | bytes 3145732
  130.3 6.2 %copy-start.15 = (bf16[128,4096]{1,0:T(8,128)(2,1)S(1)}, bf16[128,4096]{1,0:T(8,128)(2,1)}, u32[]{:S(2)}) copy-start(bf16[128,4096]{1,0:T(8,128)(2,1)} %copy-done.14) | copy-start | bytes 3145732
  130.3 29.0 %all-to-all-start.3 = ((bf16[16,256,128]{2,1,0:T(8,128)(2,1)}), bf16[16,256,128]{2,1,0:T(8,128)(2,1)S(1)}, u32[]{:S(2)}, u32[]{:S(2)}) async-start(bf16[16,256,128]{2,1,0:T(8,128)(2,1)} %get-tuple-element.41), calls=%async_computation.3 | async-start | bytes 2097152 | tf_op jit(solution)/shard_map/all_to_all | solution.py:258
  150.8 15.8 %copy-start.7 = (bf16[128,4096]{1,0:T(8,128)(2,1)S(1)}, bf16[128,4096]{1,0:T(8,128)(2,1)}, u32[]{:S(2)}) copy-start(bf16[128,4096]{1,0:T(8,128)(2,1)} %cotangent_ref.3) | copy-start | bytes 3145732
  150.8 40.9 %collective-permute-start.1 = (bf16[4096,128]{1,0:T(8,128)(2,1)}, bf16[4096,128]{1,0:T(8,128)(2,1)}, u32[]{:S(2)}, u32[]{:S(2)}) collective-permute-start(bf16[4096,128]{1,0:T(8,128)(2,1)} %get-tuple-element.37.grad_mixed_ref), channel_id=1, source_target_pairs={{2,0},{4,2},{6,4},{8,6},{10,8},{12,10},{14,12},{16,14},{18,16},{20... | collective-permute-start | bytes 3145736 | tf_op jit(solution)/shard_map/ppermute | solution.py:356
  160.1 28.8 %all-to-all-start.4 = ((f32[16,16,256]{2,1,0:T(8,128)}), f32[16,16,256]{2,1,0:T(8,128)}, u32[]{:S(2)}, u32[]{:S(2)}) async-start(f32[16,16,256]{2,1,0:T(8,128)} %pad_maximum_fusion), calls=%async_computation.4 | async-start | bytes 524288 | tf_op jit(solution)/shard_map/all_to_all | solution.py:258
  166.6 30.2 %copy-start.11 = (bf16[128,4096]{1,0:T(8,128)(2,1)S(1)}, bf16[128,4096]{1,0:T(8,128)(2,1)}, u32[]{:S(2)}) copy-start(bf16[128,4096]{1,0:T(8,128)(2,1)} %values_ref.3) | copy-start | bytes 3145732
  172.4 24.4 %copy-start.9 = (bf16[128,4096]{1,0:T(8,128)(2,1)S(1)}, bf16[128,4096]{1,0:T(8,128)(2,1)}, u32[]{:S(2)}) copy-start(bf16[128,4096]{1,0:T(8,128)(2,1)} %first_ref.3) | copy-start | bytes 3145732
  192.5 20.8 %all-to-all-start.5 = ((f32[32,17,128]{2,1,0:T(8,128)}), f32[32,17,128]{2,1,0:T(8,128)}, u32[]{:S(2)}, u32[]{:S(2)}) async-start(f32[32,17,128]{2,1,0:T(8,128)} %broadcast_in_dim.2), calls=%async_computation.5 | async-start | bytes 786432 | tf_op jit(solution)/shard_map/all_to_all | solution.py:393
